TPU v7x, 32 devices: a whole 2x2x4 slice. The times are simulated.
32 devices in a mesh: seq: 8 (over z, y), head: 2 (over x), dp: 2 (over core).
Axes of the slice: x: 2, y: 2, z: 4, core: 2. Of those that a mesh axis runs over, the one named last changes fastest.
Arguments:
- activations: bfloat16 [2, 8192, 1024], P('dp', 'seq'), may hold values from -16 to 16
- project_weight: bfloat16 [1024, 3, 1024], P(None, None, 'head'), may hold values from -0.1875 to 0.1875
- merge_weight: bfloat16 [1024, 1024], P('head'), may hold values from -0.1875 to 0.1875
- cotangent: bfloat16 [2, 8192, 1024], P('dp', 'seq'), may hold values from -6 to 6
Outputs:
- attention_out: bfloat16 [2, 8192, 1024], P('dp', 'seq', 'head')
- grad_activations: bfloat16 [2, 8192, 1024], P('dp', 'seq', 'head')
- grad_project: float32 [1024, 3, 1024], P('seq', None, ('head', 'dp'))
- grad_merge: float32 [1024, 1024], P('head', ('seq', 'dp'))
All inputs are finite; a program needn't handle non-finite values.
Results may differ from a plain program's by a relative error of at most 0.0079.
Values may be sent and summed in bfloat16 or wider, within the bound.
A program may use at most 192 MiB of HBM per device.

v0:
```python
import math

import jax
import jax.numpy as jnp
from jax import lax
from jax.sharding import PartitionSpec as P

DH = 64
BLOCK = 128
POOL = 8


EPSILON = 1e-06
HIGHEST = lax.Precision.HIGHEST
PAIR_FACTORS = (0.5, 1.0 / math.sqrt(2.0))


def partner_2(value, axis, apart):
    mask = 2**apart
    pairs = [(source, source ^ mask) for source in range(lax.axis_size(axis))]
    return lax.ppermute(value, axis, pairs)


def for_sending(x):

    def short(part):
        return part.astype(jnp.bfloat16) if part.dtype == jnp.float32 else part

    return jax.tree.map(short, x)


def unit_rows(vectors):
    return vectors * lax.rsqrt(jnp.mean(vectors * vectors, axis=-1, keepdims=True) + EPSILON)


def pool_tokens(key_rows, value_rows, window):
    token_count, head_count, head_size = key_rows.shape
    pool_shape = (token_count // window, window, head_count, head_size)
    pooled_keys = key_rows.astype(jnp.float32).reshape(pool_shape).mean(axis=1)
    pooled_values = value_rows.astype(jnp.float32).reshape(pool_shape).sum(axis=1) * (
        1.0 / math.sqrt(window)
    )
    return (pooled_keys, pooled_values)


def sibling_blocks(pooled, entries, block_count):
    groups = pooled.shape[0] // entries
    trailing = pooled.shape[1:]
    grouped = pooled.reshape((groups // 2, 2, entries) + trailing)[:, ::-1]
    grouped = grouped.reshape((groups, 1, entries) + trailing)
    spread = jnp.broadcast_to(grouped, (groups, block_count // groups, entries) + trailing)
    return spread.reshape((block_count, entries) + trailing)


def block_scores(queries, key_rows, block_len):
    token_count, head_count, head_size = queries.shape
    block_shape = (token_count // block_len, block_len, head_count, head_size)
    scores = jnp.einsum(
        "bqhe,bkhe->bhqk",
        queries.reshape(block_shape),
        key_rows.reshape(block_shape),
        preferred_element_type=jnp.float32,
    )
    return scores * (1.0 / math.sqrt(head_size))


def fine_back(grad_fine, queries, key_rows, block_len):
    token_count, head_count, head_size = queries.shape
    block_shape = (token_count // block_len, block_len, head_count, head_size)
    score_scale = 1.0 / math.sqrt(head_size)
    grad_q = (
        jnp.einsum("bhqk,bkhe->bqhe", grad_fine, key_rows.reshape(block_shape), precision=HIGHEST)
        * score_scale
    )
    grad_k = (
        jnp.einsum("bhqk,bqhe->bkhe", grad_fine, queries.reshape(block_shape), precision=HIGHEST)
        * score_scale
    )
    return (
        grad_q.reshape(token_count, head_count, head_size),
        grad_k.reshape(token_count, head_count, head_size),
    )


def attend(
    queries, key_rows, value_rows, fine_scores, far_keys, far_values, block_len, window, rounded
):
    token_count, head_count, head_size = queries.shape
    block_count = token_count // block_len
    entries = block_len // window
    coarse_keys = []
    coarse_values = []
    for level_index in range(block_count.bit_length() - 1):
        pooled_keys, pooled_values = pool_tokens(key_rows, value_rows, window << level_index)
        coarse_keys.append(sibling_blocks(pooled_keys, entries, block_count))
        coarse_values.append(sibling_blocks(pooled_values, entries, block_count))
    for level_keys, level_values in zip(far_keys, far_values):
        coarse_keys.append(jnp.broadcast_to(level_keys[None], (block_count,) + level_keys.shape))
        coarse_values.append(
            jnp.broadcast_to(level_values[None], (block_count,) + level_values.shape)
        )
    score_scale = 1.0 / math.sqrt(head_size)
    block_shape = (block_count, block_len, head_count, head_size)
    query_blocks = queries.reshape(block_shape)
    value_blocks = value_rows.reshape(block_shape)
    fine_exp = jnp.exp(fine_scores)
    all_keys = jnp.concatenate(coarse_keys, axis=1)
    all_values = jnp.concatenate(coarse_values, axis=1)
    coarse_scores = (
        jnp.einsum("bqhe,bche->bhqc", query_blocks.astype(jnp.float32), all_keys, precision=HIGHEST)
        * score_scale
    )
    coarse_exp = jnp.exp(coarse_scores)
    denominator = jnp.sum(fine_exp, axis=-1) + jnp.sum(coarse_exp, axis=-1)
    inverse = 1.0 / denominator
    fine_weights = fine_exp * inverse[..., None]
    if rounded:
        combined = jnp.einsum(
            "bhqk,bkhe->bqhe",
            fine_weights.astype(jnp.bfloat16),
            value_blocks,
            preferred_element_type=jnp.float32,
        )
    else:
        combined = jnp.einsum("bhqk,bkhe->bqhe", fine_weights, value_blocks, precision=HIGHEST)
    combined = combined + jnp.einsum(
        "bhqc,bche->bqhe", coarse_exp * inverse[..., None], all_values, precision=HIGHEST
    )
    return combined.reshape(token_count, head_count, head_size)


def pair_factors():
    return jnp.array(PAIR_FACTORS, jnp.float32)[:, None, None]


def pair_stack(stacked):
    half_count = stacked.shape[1] // 2
    return stacked.reshape(2, half_count, 2, stacked.shape[2]).sum(axis=2) * pair_factors()


def local(activations, project_weight, merge_weight, cotangent):
    token_count = activations.shape[1]
    model_width = activations.shape[2]
    local_cols = project_weight.shape[2]
    head_count = local_cols // DH
    entries = BLOCK // POOL
    token_rows = activations[0]
    flat_weight = project_weight.reshape(model_width, 3 * local_cols)
    projected = jnp.dot(token_rows, flat_weight, preferred_element_type=jnp.float32).reshape(
        token_count, 3, head_count, DH
    )
    query_raw = projected[:, 0]
    key_raw = projected[:, 1]
    query_unit = unit_rows(query_raw).astype(jnp.bfloat16)
    key_unit = unit_rows(key_raw).astype(jnp.bfloat16)
    value_round = projected[:, 2].astype(jnp.bfloat16)
    fine_scores = block_scores(query_unit, key_unit, BLOCK)

    def shard_pool(key_input, value_input):
        pooled_keys, pooled_values = pool_tokens(key_input, value_input, token_count // entries)
        return jnp.stack(
            [pooled_keys.reshape(entries, local_cols), pooled_values.reshape(entries, local_cols)]
        )

    own_stack = shard_pool(key_unit, value_round)
    bit_count = lax.axis_size("seq").bit_length() - 1
    seq_index = lax.axis_index("seq")
    uppers = [seq_index >> level_index & 1 == 1 for level_index in range(bit_count)]
    received = []
    current = own_stack
    for level_index in range(bit_count):
        partner = partner_2(current, "seq", level_index)
        received.append(partner)
        if level_index + 1 < bit_count:
            upper_side = uppers[level_index]
            lower_half = jnp.where(upper_side, partner, current)
            upper_half = jnp.where(upper_side, current, partner)
            current = pair_stack(jnp.concatenate([lower_half, upper_half], axis=1))
    far_keys = [sibling[0].reshape(entries, head_count, DH) for sibling in received]
    far_values = [sibling[1].reshape(entries, head_count, DH) for sibling in received]
    attended = attend(
        query_unit, key_unit, value_round, fine_scores, far_keys, far_values, BLOCK, POOL, True
    )
    attended_round = attended.astype(jnp.bfloat16).reshape(token_count, local_cols)
    partial_out = jnp.dot(attended_round, merge_weight, preferred_element_type=jnp.float32)
    attention_out = lax.psum_scatter(partial_out, "head", scatter_dimension=1, tiled=True).astype(
        jnp.bfloat16
    )[None]
    cotangent_rows = cotangent[0]
    grad_attended = jnp.einsum(
        "td,cd->tc", cotangent_rows, merge_weight, preferred_element_type=jnp.float32
    ).astype(jnp.bfloat16)
    out_term = jnp.einsum(
        "tc,td->cd", attended_round, cotangent_rows, preferred_element_type=jnp.float32
    )
    grad_merge = lax.psum_scatter(out_term, ("seq", "dp"), scatter_dimension=1, tiled=True)

    def attention_map(query_input, key_input, value_input, fine_input, keys_far, values_far):
        return attend(
            query_input,
            key_input,
            value_input,
            fine_input,
            keys_far,
            values_far,
            BLOCK,
            POOL,
            False,
        )

    query_full = query_unit.astype(jnp.float32)
    key_full = key_unit.astype(jnp.float32)
    value_full = value_round.astype(jnp.float32)
    _, attention_pull = jax.vjp(
        attention_map, query_full, key_full, value_full, fine_scores, far_keys, far_values
    )
    grad_query, grad_key, grad_value, grad_fine, grad_far_keys, grad_far_values = attention_pull(
        grad_attended.astype(jnp.float32).reshape(token_count, head_count, DH)
    )
    fine_query, fine_key = fine_back(grad_fine, query_full, key_full, BLOCK)
    grad_query = grad_query + fine_query
    grad_key = grad_key + fine_key
    grad_far = [
        jnp.stack(
            [level_keys.reshape(entries, local_cols), level_values.reshape(entries, local_cols)]
        )
        for level_keys, level_values in zip(grad_far_keys, grad_far_values)
    ]
    carried = jnp.zeros_like(own_stack)
    for level_index in reversed(range(bit_count)):
        upper_side = uppers[level_index]
        spread = jnp.repeat(carried * pair_factors(), 2, axis=1)
        lower_grad = spread[:, :entries]
        upper_grad = spread[:, entries:]
        own_grad = jnp.where(upper_side, upper_grad, lower_grad)
        partner_grad = jnp.where(upper_side, lower_grad, upper_grad)
        returned = partner_2(for_sending(partner_grad + grad_far[level_index]), "seq", level_index)
        carried = own_grad + returned
    _, pool_pull = jax.vjp(shard_pool, key_full, value_full)
    pool_key, pool_value = pool_pull(carried)
    grad_key = grad_key + pool_key
    grad_value = grad_value + pool_value
    _, query_pull = jax.vjp(unit_rows, query_raw)
    (grad_query_raw,) = query_pull(grad_query)
    _, key_pull = jax.vjp(unit_rows, key_raw)
    (grad_key_raw,) = key_pull(grad_key)
    grad_projected = jnp.stack([grad_query_raw, grad_key_raw, grad_value], axis=1).astype(
        jnp.bfloat16
    )
    grad_projected = grad_projected.reshape(token_count, 3, local_cols)
    input_term = jnp.einsum(
        "tjc,djc->td", grad_projected, project_weight, preferred_element_type=jnp.float32
    )
    grad_activations = lax.psum_scatter(input_term, "head", scatter_dimension=1, tiled=True).astype(
        jnp.bfloat16
    )[None]
    data_count = lax.axis_size("dp")
    part_cols = local_cols // data_count
    shard_count = lax.axis_size("seq")
    shard_rows = model_width // shard_count
    row_blocks = token_rows.reshape(token_count, shard_count, shard_rows)
    column_parts = grad_projected.reshape(token_count, 3, data_count, part_cols)
    weight_term = jnp.einsum(
        "tsr,tjhc->shrjc", row_blocks, column_parts, preferred_element_type=jnp.float32
    )
    weight_term = weight_term.reshape(shard_count * data_count * shard_rows, 3, part_cols)
    grad_project = lax.psum_scatter(weight_term, ("seq", "dp"), scatter_dimension=0, tiled=True)
    return (attention_out, grad_activations, grad_project, grad_merge)


def solution(mesh):
    return jax.shard_map(
        local,
        mesh=mesh,
        in_specs=(
            P("dp", "seq", None),
            P(None, None, "head"),
            P("head", None),
            P("dp", "seq", None),
        ),
        out_specs=(
            P("dp", "seq", "head"),
            P("dp", "seq", "head"),
            P("seq", None, ("head", "dp")),
            P("head", ("seq", "dp")),
        ),
        check_vma=False,
    )
```

profile of v0, /device:TPU:0, one launch (start us, length us, event | category | flops | bytes accessed | tf_op | source)
XLA Modules:
  0.0 617.5 jit_solution(4836803200047620773)
XLA Ops:
  7.2 4.8 copy.252
  12.0 6.0 fusion.29
  31.5 4.5 squeeze.33
  48.3 3.9 copy.255
  65.6 3.7 reduce_sum.289
  99.3 3.9 multiply_reduce_fusion
  132.8 9.0 %concatenate.21 = f32[8,96,8,64]{1,3,2,0:T(8,128)} concatenate(f32[8,16,8,64]{1,3,2,0:T(8,128)} %bitcast.293, f32[8,16,8,64]{1,3,2,0:T(8,128)} %bitcast.300, f32[8,16,8,64]{1,3,2,0:T(8,128)} %bitcast.295, f32[8,16,8,64]{1,3,2,0:T(8,128)} %broadcast_in_dim.93, f32[8,16,8,64]{1,3,2,0:T(8,128)} %broadcast_in_dim.95, f32[8,16,8,64]{1,3,2,0:T(8,128)} %broadcast_in_dim.97), dimensions={1} | concatenate | bytes 3145728 | tf_op jit(solution)/shard_map/concatenate | solution.py:108
  141.8 6.0 fusion.74
  155.8 17.5 %concatenate.20 = f32[8,96,8,64]{1,3,2,0:T(8,128)} concatenate(f32[8,16,8,64]{1,3,2,0:T(8,128)} %bitcast.294, f32[8,16,8,64]{1,3,2,0:T(8,128)} %bitcast.301, f32[8,16,8,64]{1,3,2,0:T(8,128)} %bitcast.296, f32[8,16,8,64]{1,3,2,0:T(8,128)} %broadcast_in_dim.83, f32[8,16,8,64]{1,3,2,0:T(8,128)} %broadcast_in_dim.85, f32[8,16,8,64]{1,3,2,0:T(8,128)} %broadcast_in_dim.87), dimensions={1} | concatenate | bytes 3145728 | tf_op jit(solution)/shard_map/concatenate | solution.py:107
  173.3 5.9 multiply_reduce_fusion.1
  182.5 3.8 convolution_bitcast_fusion
  186.3 4.1 slice_reduce_fusion.5
  207.9 5.0 fusion.47
  218.2 8.0 %slice_reduce_fusion.4 = (bf16[16,8,64]{0,2,1:T(8,128)(2,1)S(1)}, f32[16,8,64]{0,2,1:T(8,128)}, f32[16,8,64]{0,2,1:T(8,128)}, f32[8,16,8,64]{1,3,2,0:T(8,128)}) fusion(f32[8,96,8,64]{1,3,2,0:T(8,128)} %copy-done.4), kind=kLoop, calls=%fused_computation.51 | loop fusion | flops 172032 | bytes 1392640 | tf_op jit(solution)/shard_map/transpose(jvp())/reduce_sum | solution.py:100
  242.1 5.5 fusion.50
  247.6 6.2 %multiply_bitcast_fusion = (f32[8,8,8,8,128]{4,3,2,1,0:T(8,128)}, f32[8,128,8,64]{1,3,2,0:T(8,128)}) fusion(bf16[8,128,8,64]{1,3,2,0:T(8,128)(2,1)S(1)} %copy-done.17, f32[8,8,128,128]{2,3,1,0:T(8,128)S(1)} %copy-done.13, f32[8,8,128,128]{2,3,1,0:T(8,128)S(1)} %copy-done.3, f32[8,8,128]{2,1,0:T(8,128)S(1)} %get-tuple-element.32, ...), kind=kOutput, calls=%fused_computation.84 | convolution fusion | flops 810024960 | bytes 13697024 | tf_op jit(solution)/shard_map/bhqk,bqhe->bkhe/dot_general | solution.py:76
  257.3 4.8 bitcast_add_fusion.1
  274.5 3.9 copy.346
  278.4 4.9 reshape.601
  283.4 4.1 copy.295
  290.2 4.1 copy.286
  299.4 4.8 reshape.585
  306.5 3.9 copy.293
  310.3 3.9 copy.306
  316.5 4.8 reshape.583
  323.6 3.8 copy.291
  327.4 3.9 copy.305
  333.6 4.8 reshape.581
  340.7 3.8 copy.290
  344.5 3.8 copy.304
  351.3 5.1 reshape.578
  356.3 4.9 reshape.573
  364.0 4.9 reshape.602
  371.8 7.9 %fusion.28 = (f32[1024,8]{0,1:T(8,128)S(1)}, f32[1024,8]{0,1:T(8,128)S(1)}) fusion(f32[1024,3,8,64]{0,3,2,1:T(8,128)} %copy-done.10, f32[1024,8,64]{0,2,1:T(8,128)} %reshape.578, f32[8,8,8,8,128]{4,3,2,1,0:T(8,128)} %get-tuple-element.22, f32[1024,8,64]{0,2,1:T(8,128)} %copy.306, f32[1024,8,64]{0,2,1:T(8,128)} %copy.304, f32[1024,8,64]{0,2,1:T(8,128)} %copy.305, ...), kind=kLoop, calls=%fused_computation.46 | loop fusion | flops 4177920 | bytes 16842752 | tf_op jit(solution)/shard_map/transpose(jvp())/reduce_sum | solution.py:33
  381.3 6.2 %fusion.22 = (bf16[1024,1,8,64]{0,3,2,1:T(8,128)(2,1)S(1)}, bf16[1024,1,8,64]{0,3,2,1:T(8,128)(2,1)}) fusion(f32[1024,1,8,64]{0,3,2,1:T(8,128)} %add.135, f32[1024,8]{0,1:T(8,128)S(1)} %get-tuple-element.47, f32[1024,8]{0,1:T(8,128)S(1)} %copy-done.61, f32[1024,3,8,64]{0,3,2,1:T(8,128)S(1)} %bitcast.271, f32[1024,8]{0,1:T(8,128)S(1)} %get-tuple-element.46, ...), kind=kLoop, calls=%fused_computation.38 | loop fusion | flops 7340032 | bytes 19005440 | tf_op jit(solution)/shard_map/convert.13
  391.1 5.3 add_convert_fusion
  396.6 5.0 fusion.19
  402.0 3.8 fusion.31
  405.9 4.0 copy.349
  409.8 4.1 copy.310
  414.0 5.3 reshape.590
  419.2 5.5 reshape.589
  424.7 5.5 reshape.588
  435.9 4.9 reshape.591
  447.2 4.9 fusion.38
  452.5 3.8 fusion.17
  465.2 56.2 %reduce-scatter.11.cloned.1.call-done = f32[512,64]{0,1:T(8,128)} async-done(((f32[512,1024]{0,1:T(8,128)}), f32[512,64]{0,1:T(8,128)}) %reduce-scatter.11.cloned.1.call-update) | async-done | bytes 131088 | tf_op jit(solution)/shard_map/reduce_scatter | solution.py:196
  521.3 89.2 %reduce-scatter.9.cloned.1.call-done = f32[128,3,256]{2,0,1:T(8,128)} async-done(((f32[2048,3,256]{2,0,1:T(8,128)}), f32[128,3,256]{2,0,1:T(8,128)}) %reduce-scatter.9.cloned.1.call-update) | async-done | bytes 393232 | tf_op jit(solution)/shard_map/reduce_scatter | solution.py:267
  (286 shorter events, 219.1 us)
Async XLA Ops:
  7.2 45.0 %copy-start = (bf16[1,1024,1024]{2,1,0:T(8,128)(2,1)S(1)}, bf16[1,1024,1024]{2,1,0:T(8,128)(2,1)}, u32[]{:S(2)}) copy-start(bf16[1,1024,1024]{2,1,0:T(8,128)(2,1)} %param.12) | copy-start | bytes 6291460
  7.2 452.6 %reduce-scatter.5.cloned.1.call-start = ((), (), s32[]{:S(2)}) async-start(), calls=%async_computation.4 | async-start | bytes 6291456 | tf_op jit(solution)/shard_map/reduce_scatter | solution.py:186
  18.6 4.4 copy-start.55
  18.6 39.2 %copy-start.57 = (f32[1024,8]{0,1:T(8,128)}, f32[1024,8]{0,1:T(8,128)S(1)}, u32[]{:S(2)}) copy-start(f32[1024,8]{0,1:T(8,128)S(1)} %get-tuple-element.7) | copy-start | bytes 98308
  20.7 24.8 %copy-start.22 = (bf16[1024,1,8,64]{0,3,2,1:T(8,128)(2,1)}, bf16[1024,1,8,64]{0,3,2,1:T(8,128)(2,1)S(1)}, u32[]{:S(2)}) copy-start(bf16[1024,1,8,64]{0,3,2,1:T(8,128)(2,1)S(1)} %slice.85) | copy-start | bytes 3145732
  31.5 4.5 copy-start.60
  41.5 65.5 %collective-permute-start = (f32[2,16,512]{2,0,1:T(2,128)}, f32[2,16,512]{2,0,1:T(2,128)}, u32[]{:S(2)}, u32[]{:S(2)}) collective-permute-start(f32[2,16,512]{2,0,1:T(2,128)} %pad_maximum_fusion.2), channel_id=1, source_target_pairs={{0,4},{4,0},{8,12},{12,8},{16,20},{20,16},{24,28},{28,24},{1,5},{5... | collective-permute-start | bytes 196616 | tf_op jit(solution)/shard_map/ppermute | solution.py:21
  79.1 5.4 copy-start.29
  98.8 4.3 copy-start.1
  103.1 4.9 copy-start.65
  108.7 4.9 collective-permute-start.1
  115.4 5.5 collective-permute-start.2
  141.7 6.0 copy-start.31
  173.2 5.9 copy-start.63
  173.2 5.9 copy-start.64
  173.3 6.0 copy-start.2
  173.3 6.0 copy-start.25
  179.1 11.2 %copy-start.7 = (f32[8,8,128,96]{2,3,1,0:T(8,128)}, f32[8,8,128,96]{2,3,1,0:T(8,128)S(1)}, u32[]{:S(2)}) copy-start(f32[8,8,128,96]{2,3,1,0:T(8,128)S(1)} %get-tuple-element.44) | copy-start | bytes 9437188
  198.8 263.6 %reduce-scatter.7.cloned.1.call-start = ((), (), s32[]{:S(2)}) async-start(), calls=%async_computation.5 | async-start | bytes 6291456 | tf_op jit(solution)/shard_map/reduce_scatter | solution.py:254
  227.0 38.9 %collective-permute-start.3 = (bf16[2,16,512]{2,0,1:T(2,128)(2,1)}, bf16[2,16,512]{2,0,1:T(2,128)(2,1)}, u32[]{:S(2)}, u32[]{:S(2)}) collective-permute-start(bf16[2,16,512]{2,0,1:T(2,128)(2,1)} %maximum_convert_fusion), channel_id=1, source_target_pairs={{0,16},{4,20},{8,24},{12,28},{16,0},{20,4},{24,8},{28,12},{1,17},{... | collective-permute-start | bytes 98312 | tf_op jit(solution)/shard_map/ppermute | solution.py:21
  233.5 7.1 %copy-start.5 = (f32[8,96,8,64]{1,3,2,0:T(8,128)S(1)}, f32[8,96,8,64]{1,3,2,0:T(8,128)}, u32[]{:S(2)}) copy-start(f32[8,96,8,64]{1,3,2,0:T(8,128)} %copy-done.4) | copy-start | bytes 4718596
  237.5 4.6 copy-start.3
  242.1 5.5 copy-start.13
  242.1 5.5 copy-start.17
  247.6 6.3 %copy-start.20 = (f32[64,8,8,128]{3,2,1,0:T(8,128)S(1)}, f32[64,8,8,128]{3,2,1,0:T(8,128)}, u32[]{:S(2)}) copy-start(f32[64,8,8,128]{3,2,1,0:T(8,128)} %copy.355) | copy-start | bytes 6291460
  257.3 4.8 copy-start.44
  257.3 5.6 copy-start.37
  262.1 9.3 %copy-start.36 = (f32[2,16,8,64]{1,3,2,0:T(8,128)S(1)}, f32[2,16,8,64]{1,3,2,0:T(8,128)}, u32[]{:S(2)}) copy-start(f32[2,16,8,64]{1,3,2,0:T(8,128)} %bitcast_reduce_fusion.1) | copy-start | bytes 196612
  263.7 8.6 %copy-start.41 = (f32[16,8,64]{0,2,1:T(8,128)S(1)}, f32[16,8,64]{0,2,1:T(8,128)}, u32[]{:S(2)}) copy-start(f32[16,8,64]{0,2,1:T(8,128)} %get-tuple-element.16) | copy-start | bytes 98308
  267.5 4.9 collective-permute-start.4
  272.7 75.7 %collective-permute-start.5 = (bf16[2,16,512]{2,0,1:T(2,128)(2,1)S(1)}, bf16[2,16,512]{2,0,1:T(2,128)(2,1)S(1)}, u32[]{:S(2)}, u32[]{:S(2)}) collective-permute-start(bf16[2,16,512]{2,0,1:T(2,128)(2,1)S(1)} %fusion.80), channel_id=1, source_target_pairs={{0,4},{4,0},{8,12},{12,8},{16,20},{20,16},{24,28},{28,24},{1,5},{5... | collective-permute-start | bytes 98312 | tf_op jit(solution)/shard_map/ppermute | solution.py:21
  299.4 4.9 copy-start.38
  371.7 8.0 %slice-start = ((s8[6291456]{0:T(1024)(128)(4,1)}), s8[4194304]{0:T(1024)(128)(4,1)S(1)}, s32[]{:S(2)}) async-start(s8[6291456]{0:T(1024)(128)(4,1)} %bitcast.270), calls=%async_computation.8 | async-start | bytes 8388608
  371.7 7.9 %copy-start.56 = (f32[1024,8]{0,1:T(8,128)S(1)}, f32[1024,8]{0,1:T(8,128)}, u32[]{:S(2)}) copy-start(f32[1024,8]{0,1:T(8,128)} %copy-done.55) | copy-start | bytes 98308
  371.7 7.9 %copy-start.58 = (f32[1024,8]{0,1:T(8,128)S(1)}, f32[1024,8]{0,1:T(8,128)}, u32[]{:S(2)}) copy-start(f32[1024,8]{0,1:T(8,128)} %copy-done.57) | copy-start | bytes 98308
  371.7 8.0 %slice-start.1 = ((s8[6291456]{0:T(1024)(128)(4,1)}), s8[2097152]{0:T(1024)(128)(4,1)S(1)}, s32[]{:S(2)}) async-start(s8[6291456]{0:T(1024)(128)(4,1)} %bitcast.270), calls=%async_computation.9 | async-start | bytes 4194304
  371.7 8.3 %copy-start.26 = (f32[1024,1,8,64]{0,3,2,1:T(8,128)S(1)}, f32[1024,1,8,64]{0,3,2,1:T(8,128)}, u32[]{:S(2)}) copy-start(f32[1024,1,8,64]{0,3,2,1:T(8,128)} %copy.293) | copy-start | bytes 6291460
  371.7 8.9 %copy-start.27 = (f32[1024,1,8,64]{0,3,2,1:T(8,128)S(1)}, f32[1024,1,8,64]{0,3,2,1:T(8,128)}, u32[]{:S(2)}) copy-start(f32[1024,1,8,64]{0,3,2,1:T(8,128)} %copy.291) | copy-start | bytes 6291460
  371.8 9.5 %copy-start.28 = (f32[1024,1,8,64]{0,3,2,1:T(8,128)S(1)}, f32[1024,1,8,64]{0,3,2,1:T(8,128)}, u32[]{:S(2)}) copy-start(f32[1024,1,8,64]{0,3,2,1:T(8,128)} %copy.290) | copy-start | bytes 6291460
  371.8 9.5 %copy-start.61 = (f32[1024,8]{0,1:T(8,128)S(1)}, f32[1024,8]{0,1:T(8,128)}, u32[]{:S(2)}) copy-start(f32[1024,8]{0,1:T(8,128)} %get-tuple-element.40) | copy-start | bytes 98308
  391.1 5.3 copy-start.33
  391.1 5.3 copy-start.51
  391.1 5.5 copy-start.52
  401.7 119.7 %reduce-scatter.11.cloned.1.call-start = ((), (), s32[]{:S(2)}) async-start(), calls=%async_computation.7 | async-start | bytes 2228224 | tf_op jit(solution)/shard_map/reduce_scatter | solution.py:196
  405.8 204.7 %reduce-scatter.9.cloned.1.call-start = ((), (), s32[]{:S(2)}) async-start(), calls=%async_computation.6 | async-start | bytes 6684672 | tf_op jit(solution)/shard_map/reduce_scatter | solution.py:267
  447.2 4.9 copy-start.40
  447.2 5.0 copy-start.49
  447.2 5.3 copy-start.50
  (30 other events, 86.2 us)
Sparse Core Ops, SparseCore 0:
  198.9 54.9 reduce-scatter.4
  401.8 53.6 reduce-scatter.6
  459.8 61.5 reduce-scatter.10
  526.2 84.2 reduce-scatter.8
where the time goes:
time: 629 us; the launch traced here: 617 us
  local copies, waits for them, and re-layouts  273 us (43%)
  waiting for transfers between devices  146 us (23%)
  other arithmetic  97.4 us (15%)
  matrix products  73.7 us (12%)
  between operations  15 us (2%)
  starting transfers between devices  12.5 us (2%)
    reduce_scatter x1, waiting for transfers between devices, local(): lax.psum_scatter(weight_term, ('seq', 'dp'), scatter_dimension=0, tiled=T...  89.2 us
    reduce_scatter x1, waiting for transfers between devices, local(): lax.psum_scatter(out_term, ('seq', 'dp'), scatter_dimension=1, tiled=True)  56.2 us
    reshape x10, local copies, waits for them, and re-layouts, pool_tokens(): value_rows.astype(jnp.float32).reshape(pool_shape).sum(axis=1)  46.1 us
    reshape x8, local copies, waits for them, and re-layouts, pool_tokens(): pooled_keys = key_rows.astype(jnp.float32).reshape(pool_shape).mean(axis=1)  33.1 us
    unnamed x141, local copies, waits for them, and re-layouts  23.8 us
    concatenate x1, local copies, waits for them, and re-layouts, attend(): all_keys = jnp.concatenate(coarse_keys, axis=1)  17.5 us
    another operation x3, other arithmetic  16.4 us
    broadcast_in_dim x8, local copies, waits for them, and re-layouts, sibling_blocks(): jnp.broadcast_to(grouped, (groups, block_count // groups, entries) + trai...  15.2 us
  transfers between devices with their start and end apart: 10, of which 3 were waited for; matrix products, arithmetic and copies ran while one was open for 52% of the time, Pallas kernels for 0%

commit v1 on v0

v1 whole, which is shorter than its diff:
```python
import functools
import math

import jax
import jax.numpy as jnp
from jax import lax
from jax.experimental import pallas as pl
from jax.experimental.pallas import tpu as pltpu
from jax.sharding import PartitionSpec as P

DH = 64
BLOCK = 128
POOL = 8
ENTRIES = BLOCK // POOL
LANES = 2 * DH
EPSILON = 1e-06
F32 = jnp.float32
BF16 = jnp.bfloat16
PAIR_FACTORS = (0.5, 1.0 / math.sqrt(2.0))
VMEM_LIMIT = 48 * 1024 * 1024


def dot_nn(a, b):
    return lax.dot_general(a, b, (((1,), (0,)), ((), ())), preferred_element_type=F32)


def dot_nt(a, b):
    return lax.dot_general(a, b, (((1,), (1,)), ((), ())), preferred_element_type=F32)


def dot_tn(a, b):
    return lax.dot_general(a, b, (((0,), (0,)), ((), ())), preferred_element_type=F32)


def low_half(rows):
    return lax.broadcasted_iota(jnp.int32, (rows, LANES), 1) < DH


def half_sums(x, low):
    zero = jnp.zeros_like(x)
    first = jnp.sum(jnp.where(low, x, zero), axis=1, keepdims=True)
    second = jnp.sum(jnp.where(low, zero, x), axis=1, keepdims=True)
    return first, second


def half_means(x, low):
    first, second = half_sums(x, low)
    return jnp.where(low, first, second) * (1.0 / DH)


def pool_matrix(tokens, window):
    entry = lax.broadcasted_iota(jnp.int32, (ENTRIES, tokens), 0)
    token = lax.broadcasted_iota(jnp.int32, (ENTRIES, tokens), 1)
    return (token // window == entry).astype(BF16)


def spread_matrix(tokens, window, offset):
    token = lax.broadcasted_iota(jnp.int32, (tokens, ENTRIES), 0)
    entry = lax.broadcasted_iota(jnp.int32, (tokens, ENTRIES), 1)
    return ((token + offset) // window == entry).astype(BF16)


def project_kernel(act_ref, w_ref, q_ref, k_ref, v_ref, qi_ref, ki_ref, own_ref):
    tokens = act_ref.shape[0]
    width = w_ref.shape[2]
    chunk = min(256, tokens)
    low = low_half(chunk)
    for start in range(0, tokens, chunk):
        rows = pl.ds(start, chunk)
        act = act_ref[rows, :]
        for j, (unit_ref, inv_ref) in enumerate(((q_ref, qi_ref), (k_ref, ki_ref))):
            raw = dot_nn(act, w_ref[j])
            for at in range(0, width, LANES):
                part = raw[:, at : at + LANES]
                inv = lax.rsqrt(half_means(part * part, low) + EPSILON)
                unit_ref[rows, at : at + LANES] = (part * inv).astype(BF16)
                inv_ref[rows, at : at + LANES] = inv
        v_ref[rows, :] = dot_nn(act, w_ref[2]).astype(BF16)
    window = tokens // ENTRIES
    pool = pool_matrix(tokens, window)
    own_ref[0] = dot_nn(pool, k_ref[...]) * (1.0 / window)
    own_ref[1] = dot_nn(pool, v_ref[...]) * (1.0 / math.sqrt(window))


def project(act, weight):
    tokens, model = act.shape
    cols = weight.shape[2]
    width = 256
    col = pl.BlockSpec((tokens, width), lambda i: (0, i))
    return pl.pallas_call(
        project_kernel,
        grid=(cols // width,),
        in_specs=[
            pl.BlockSpec((tokens, model), lambda i: (0, 0)),
            pl.BlockSpec((3, model, width), lambda i: (0, 0, i)),
        ],
        out_specs=[col] * 5 + [pl.BlockSpec((2, ENTRIES, width), lambda i: (0, 0, i))],
        out_shape=[jax.ShapeDtypeStruct((tokens, cols), BF16)] * 3
        + [jax.ShapeDtypeStruct((tokens, cols), F32)] * 2
        + [jax.ShapeDtypeStruct((2, ENTRIES, cols), F32)],
        compiler_params=pltpu.CompilerParams(vmem_limit_bytes=VMEM_LIMIT),
    )(act, weight)


def attend_kernel(
    far_levels, q_ref, k_ref, v_ref, do_ref, qi_ref, far_ref, att_ref, gq_ref, dk_ref, dv_ref, gf_ref
):
    tokens = q_ref.shape[0]
    blocks = tokens // BLOCK
    levels = blocks.bit_length() - 1
    coarse = ENTRIES * (levels + far_levels)
    low = low_half(BLOCK)
    key_scale = [1.0 / (POOL << l) for l in range(levels)]
    value_scale = [1.0 / math.sqrt(POOL << l) for l in range(levels)]
    pooled_k, pooled_v = [], []
    for l in range(levels):
        span = BLOCK << l
        pool = pool_matrix(span, POOL << l)
        pooled_k.append(
            [
                (dot_nn(pool, k_ref[pl.ds(g * span, span), :]) * key_scale[l])
                for g in range(blocks >> l)
            ]
        )
        pooled_v.append(
            [
                (dot_nn(pool, v_ref[pl.ds(g * span, span), :]) * value_scale[l])
                for g in range(blocks >> l)
            ]
        )
    padding = BLOCK - coarse
    pad = [jnp.zeros((padding, LANES), F32)] if padding else []
    live = (lax.broadcasted_iota(jnp.int32, (BLOCK, BLOCK), 1) < coarse).astype(F32)
    low_b = low.astype(BF16)
    high_b = (1 - low.astype(F32)).astype(BF16)
    grad_k = [[None] * (blocks >> l) for l in range(levels)]
    grad_v = [[None] * (blocks >> l) for l in range(levels)]
    far_k = jnp.zeros((far_levels * ENTRIES, LANES), F32)
    far_v = jnp.zeros((far_levels * ENTRIES, LANES), F32)

    def add(held, l, g, value):
        held[l][g] = value if held[l][g] is None else held[l][g] + value

    for b in range(blocks):
        rows = pl.ds(b * BLOCK, BLOCK)
        unit = q_ref[rows, :]
        q = unit * jnp.asarray(0.125, BF16)
        do = do_ref[rows, :]
        kc = jnp.concatenate(
            [pooled_k[l][(b >> l) ^ 1] for l in range(levels)] + [far_ref[0]] + pad, axis=0
        ).astype(BF16)
        vc = jnp.concatenate(
            [pooled_v[l][(b >> l) ^ 1] for l in range(levels)] + [far_ref[1]] + pad, axis=0
        ).astype(BF16)
        kf, vf = k_ref[rows, :], v_ref[rows, :]
        keys = jnp.concatenate([kf * low_b, kf * high_b, kc * low_b, kc * high_b], axis=0)
        values = jnp.concatenate([vf * low_b, vf * high_b, vc * low_b, vc * high_b], axis=0)
        scores = dot_nt(q, keys)
        e = [jnp.exp(scores[:, i * BLOCK : (i + 1) * BLOCK]) for i in range(4)]
        if padding:
            e[2], e[3] = e[2] * live, e[3] * live
        inv = [1.0 / jnp.sum(e[i] + e[i + 2], axis=1, keepdims=True) for i in range(2)]
        p = [e[i] * inv[i % 2] for i in range(4)]
        pb = jnp.concatenate([part.astype(BF16) for part in p], axis=1)
        out = dot_nn(pb, values)
        att_ref[rows, :] = out.astype(BF16)
        delta = half_sums(out * do.astype(F32), low)
        dp = dot_nt(do, values)
        ds = jnp.concatenate(
            [
                (p[i] * (dp[:, i * BLOCK : (i + 1) * BLOCK] - delta[i % 2])).astype(BF16)
                for i in range(4)
            ],
            axis=1,
        )
        dq = dot_nn(ds, keys) * 0.125
        u = unit.astype(F32)
        gq_ref[rows, :] = (qi_ref[rows, :] * (dq - u * half_means(dq * u, low))).astype(BF16)
        dk = dot_tn(ds, q)
        dv = dot_tn(pb, do)
        dk_ref[rows, :] = jnp.where(low, dk[0:BLOCK], dk[BLOCK : 2 * BLOCK])
        dv_ref[rows, :] = jnp.where(low, dv[0:BLOCK], dv[BLOCK : 2 * BLOCK])
        dkc = jnp.where(low, dk[2 * BLOCK : 3 * BLOCK], dk[3 * BLOCK :])
        dvc = jnp.where(low, dv[2 * BLOCK : 3 * BLOCK], dv[3 * BLOCK :])
        for l in range(levels):
            part = slice(l * ENTRIES, (l + 1) * ENTRIES)
            add(grad_k, l, (b >> l) ^ 1, dkc[part])
            add(grad_v, l, (b >> l) ^ 1, dvc[part])
        far_k = far_k + dkc[levels * ENTRIES : coarse]
        far_v = far_v + dvc[levels * ENTRIES : coarse]
    gf_ref[0] = far_k
    gf_ref[1] = far_v
    for b in range(blocks):
        rows = pl.ds(b * BLOCK, BLOCK)
        spread = jnp.concatenate(
            [spread_matrix(BLOCK, POOL << l, (b % (1 << l)) * BLOCK) for l in range(levels)], axis=1
        )
        held_k = [grad_k[l][b >> l] * key_scale[l] for l in range(levels)]
        held_v = [grad_v[l][b >> l] * value_scale[l] for l in range(levels)]
        held_k = jnp.concatenate(held_k, axis=0).astype(BF16)
        held_v = jnp.concatenate(held_v, axis=0).astype(BF16)
        dk_ref[rows, :] += dot_nn(spread, held_k)
        dv_ref[rows, :] += dot_nn(spread, held_v)


def attend(q, k, v, do, qi, far):
    tokens, cols = q.shape
    far_levels = far.shape[1] // ENTRIES
    col = pl.BlockSpec((tokens, LANES), lambda i: (0, i))
    few = pl.BlockSpec((2, far_levels * ENTRIES, LANES), lambda i: (0, 0, i))
    return pl.pallas_call(
        functools.partial(attend_kernel, far_levels),
        grid=(cols // LANES,),
        in_specs=[col] * 5 + [few],
        out_specs=[col] * 4 + [few],
        out_shape=[jax.ShapeDtypeStruct((tokens, cols), BF16)] * 2
        + [jax.ShapeDtypeStruct((tokens, cols), F32)] * 2
        + [jax.ShapeDtypeStruct(far.shape, F32)],
        compiler_params=pltpu.CompilerParams(vmem_limit_bytes=VMEM_LIMIT),
    )(q, k, v, do, qi, far)


def finish_kernel(k_ref, ki_ref, dk_ref, dv_ref, far_ref, gk_ref, gv_ref):
    tokens = k_ref.shape[0]
    window = tokens // ENTRIES
    far_k = (far_ref[0] * (1.0 / window)).astype(BF16)
    far_v = (far_ref[1] * (1.0 / math.sqrt(window))).astype(BF16)
    chunk = min(256, tokens)
    low = low_half(chunk)
    for start in range(0, tokens, chunk):
        rows = pl.ds(start, chunk)
        spread = spread_matrix(chunk, window, start)
        g = dk_ref[rows, :] + dot_nn(spread, far_k)
        u = k_ref[rows, :].astype(F32)
        gk_ref[rows, :] = (ki_ref[rows, :] * (g - u * half_means(g * u, low))).astype(BF16)
        gv_ref[rows, :] = (dv_ref[rows, :] + dot_nn(spread, far_v)).astype(BF16)


def finish(k, ki, dk, dv, far):
    tokens, cols = k.shape
    col = pl.BlockSpec((tokens, LANES), lambda i: (0, i))
    return pl.pallas_call(
        finish_kernel,
        grid=(cols // LANES,),
        in_specs=[col] * 4 + [pl.BlockSpec((2, ENTRIES, LANES), lambda i: (0, 0, i))],
        out_specs=[col] * 2,
        out_shape=[jax.ShapeDtypeStruct((tokens, cols), BF16)] * 2,
        compiler_params=pltpu.CompilerParams(vmem_limit_bytes=VMEM_LIMIT),
    )(k, ki, dk, dv, far)


def partner_2(value, axis, apart):
    mask = 2**apart
    pairs = [(source, source ^ mask) for source in range(lax.axis_size(axis))]
    return lax.ppermute(value, axis, pairs)


def pair_factors():
    return jnp.array(PAIR_FACTORS, F32)[:, None, None]


def pair_stack(stacked):
    half_count = stacked.shape[1] // 2
    return stacked.reshape(2, half_count, 2, stacked.shape[2]).sum(axis=2) * pair_factors()


def local(activations, project_weight, merge_weight, cotangent):
    act = activations[0]
    cot = cotangent[0]
    tokens, model = act.shape
    cols = project_weight.shape[2]
    weight = jnp.moveaxis(project_weight, 1, 0)
    q, k, v, qi, ki, own = project(act, weight)
    bit_count = lax.axis_size("seq").bit_length() - 1
    seq_index = lax.axis_index("seq")
    uppers = [seq_index >> level & 1 == 1 for level in range(bit_count)]
    received = []
    current = own
    for level in range(bit_count):
        partner = partner_2(current, "seq", level)
        received.append(partner)
        if level + 1 < bit_count:
            lower_half = jnp.where(uppers[level], partner, current)
            upper_half = jnp.where(uppers[level], current, partner)
            current = pair_stack(jnp.concatenate([lower_half, upper_half], axis=1))
    do = dot_nt(cot, merge_weight).astype(BF16)
    att, gq, dk, dv, grad_far = attend(q, k, v, do, qi, jnp.concatenate(received, axis=1))
    partial_out = dot_nn(att, merge_weight).astype(BF16)
    attention_out = lax.psum_scatter(partial_out, "head", scatter_dimension=1, tiled=True)[None]
    out_term = dot_tn(att, cot)
    grad_merge = lax.psum_scatter(out_term, ("seq", "dp"), scatter_dimension=1, tiled=True)
    carried = jnp.zeros_like(own)
    for level in reversed(range(bit_count)):
        spread = jnp.repeat(carried * pair_factors(), 2, axis=1)
        lower_grad, upper_grad = spread[:, :ENTRIES], spread[:, ENTRIES:]
        own_grad = jnp.where(uppers[level], upper_grad, lower_grad)
        partner_grad = jnp.where(uppers[level], lower_grad, upper_grad)
        sent = partner_grad + grad_far[:, level * ENTRIES : (level + 1) * ENTRIES]
        carried = own_grad + partner_2(sent.astype(BF16), "seq", level)
    gk, gv = finish(k, ki, dk, dv, carried)
    grads = jnp.concatenate([gq, gk, gv], axis=1)
    flat = project_weight.reshape(model, 3 * cols)
    input_term = dot_nt(grads, flat).astype(BF16)
    grad_activations = lax.psum_scatter(input_term, "head", scatter_dimension=1, tiled=True)[None]
    data_count = lax.axis_size("dp")
    part_cols = cols // data_count
    shard_count = lax.axis_size("seq")
    shard_rows = model // shard_count
    term = dot_tn(act, grads).reshape(shard_count, shard_rows, 3, data_count, part_cols)
    term = jnp.moveaxis(term, 3, 1).reshape(model * data_count, 3, part_cols)
    grad_project = lax.psum_scatter(term, ("seq", "dp"), scatter_dimension=0, tiled=True)
    return (attention_out, grad_activations, grad_project, grad_merge)


def solution(mesh):
    return jax.shard_map(
        local,
        mesh=mesh,
        in_specs=(
            P("dp", "seq", None),
            P(None, None, "head"),
            P("head", None),
            P("dp", "seq", None),
        ),
        out_specs=(
            P("dp", "seq", "head"),
            P("dp", "seq", "head"),
            P("seq", None, ("head", "dp")),
            P("head", ("seq", "dp")),
        ),
        check_vma=False,
    )
```

time: 629 us -> 293 us (0.47); the launches traced: 617 us -> 293 us
  local copies, waits for them, and re-layouts: 273 us -> 28.7 us
  other arithmetic: 97.4 us -> 0.78 us
  matrix products: 73.7 us -> 21 us
  Pallas kernels: 0 us -> 37.5 us
  waiting for transfers between devices: 146 us -> 177 us
    reshape x25 -> x4, local copies, waits for them, and re-layouts: 103 us -> 2.16 us  [the longest x2 2.01 us: local(): spread = jnp.repeat(carried * pair_factors(), 2, axis=1)]
    reduce_scatter x3, waiting for transfers between devices: 89.2 us -> 159 us  [the longest x1 90.1 us: local(): lax.psum_scatter(term, ('seq', 'dp'), scatter_dimension=0, tiled=True)]
    broadcast_in_dim x30 -> x0, local copies, waits for them, and re-layouts: 53.3 us -> none  [the longest x8 15.2 us: sibling_blocks(): jnp.broadcast_to(grouped, (groups, block_count // groups, entries) + trai...]
    dot_general x18 -> x5, matrix products: 73.7 us -> 21 us  [the longest x2 8.66 us: dot_tn(): lax.dot_general(a, b, (((0,), (0,)), ((), ())), preferred_element_type=F32)]
    reduce_sum x16 -> x0, other arithmetic: 51.8 us -> none  [the longest x4 12.3 us: pool_tokens(): value_rows.astype(jnp.float32).reshape(pool_shape).sum(axis=1)]
    reduce_scatter x1, waiting for transfers between devices: 56.2 us -> 9.95 us  [local(): lax.psum_scatter(out_term, ('seq', 'dp'), scatter_dimension=1, tiled=True)]
    pallas_call x0 -> x3, Pallas kernels: none -> 37.5 us  [the longest x1 25 us: attend(): pl.pallas_call(functools.partial(attend_kernel, far_levels), grid=(cols /...]
    concatenate x2 -> x1, local copies, waits for them, and re-layouts: 26.4 us -> 0.07 us  [local(): grads = jnp.concatenate([gq, gk, gv], axis=1)]
  transfers between devices with their start and end apart: 10 -> 10, of which waited for: 3 -> 8; matrix products, arithmetic and copies ran while one was open for 52% -> 13% of each run, Pallas kernels for 0% -> 2%
where the time goes in v1:
time: 293 us
  waiting for transfers between devices  177 us (60%)
  Pallas kernels  37.5 us (13%)
  local copies, waits for them, and re-layouts  28.7 us (10%)
  matrix products  21 us (7%)
  between operations  14 us (5%)
  starting transfers between devices  13.5 us (5%)
    reduce_scatter x1, waiting for transfers between devices, local(): lax.psum_scatter(term, ('seq', 'dp'), scatter_dimension=0, tiled=True)  90.1 us
    reduce_scatter x1, waiting for transfers between devices, local(): lax.psum_scatter(input_term, 'head', scatter_dimension=1, tiled=True)[None]  34.7 us
    reduce_scatter x1, waiting for transfers between devices, local(): lax.psum_scatter(partial_out, 'head', scatter_dimension=1, tiled=True)[None]  33.7 us
    pallas_call x1, Pallas kernels, attend(): pl.pallas_call(functools.partial(attend_kernel, far_levels), grid=(cols /...  25 us
    unnamed x28, local copies, waits for them, and re-layouts  18.4 us
    ppermute x6, starting transfers between devices, partner_2(): return lax.ppermute(value, axis, pairs)  13.2 us
    reduce_scatter x1, waiting for transfers between devices, local(): lax.psum_scatter(out_term, ('seq', 'dp'), scatter_dimension=1, tiled=True)  9.95 us
    dot_general x2, matrix products, dot_tn(): lax.dot_general(a, b, (((0,), (0,)), ((), ())), preferred_element_type=F32)  8.66 us
  transfers between devices with their start and end apart: 10, of which 8 were waited for; matrix products, arithmetic and copies ran while one was open for 13% of the time, Pallas kernels for 2%

profile of v1, /device:TPU:0, one launch (start us, length us, event | category | flops | bytes accessed | tf_op | source)
XLA Modules:
  0.0 292.6 jit_solution(12678997281199342838)
XLA Ops:
  7.2 7.9 %shard_map.120 = (bf16[1024,512]{1,0:T(8,128)(2,1)S(1)}, bf16[1024,512]{1,0:T(8,128)(2,1)S(1)}, bf16[1024,512]{1,0:T(8,128)(2,1)S(1)}, f32[1024,512]{1,0:T(8,128...) custom-call(bf16[1024,1024]{1,0:T(8,128)(2,1)} %bitcast.35, bf16[3,1024,512]{2,1,0:T(8,128)(2,1)} %bitcast.33), custom_call_target="tpu_custom_call" | custom-call | tf_op jit(solution)/shard_map/pallas_call | solution.py:90
  15.1 1.3 copy-done.2
  16.5 1.0 copy-done.3
  17.4 1.0 copy-done.5
  18.4 3.0 %collective-permute-start = (f32[2,16,512]{2,1,0:T(8,128)S(1)}, f32[2,16,512]{2,1,0:T(8,128)S(1)}, u32[]{:S(2)}, u32[]{:S(2)}) collective-permute-start(f32[2,16,512]{2,1,0:T(8,128)S(1)} %get-tuple-element.21), channel_id=1, source_target_pairs={{0,4},{4,0},{8,12},{12,8},{16,20},{20,16},{24,28},{28,24},{1,5},{5... | collective-permute-start | bytes 196616 | tf_op jit(solution)/shard_map/ppermute | solution.py:255
  21.4 2.2 collective-permute-done
  23.6 0.1 reshape.35
  23.7 0.2 reduce_sum.18
  23.9 0.1 broadcast_multiply_fusion.1
  24.0 2.1 collective-permute-start.1
  26.1 2.2 collective-permute-done.1
  28.3 0.1 broadcast_select_fusion.1
  28.4 0.1 reshape.36
  28.5 0.2 reduce_sum.19
  28.6 0.1 broadcast_multiply_fusion
  28.7 3.1 %collective-permute-start.2 = (f32[2,16,512]{2,1,0:T(8,128)S(1)}, f32[2,16,512]{2,1,0:T(8,128)S(1)}, u32[]{:S(2)}, u32[]{:S(2)}) collective-permute-start(f32[2,16,512]{2,1,0:T(8,128)S(1)} %broadcast_multiply_fusion), channel_id=1, source_target_pairs={{0,16},{4,20},{8,24},{12,28},{16,0},{20,4},{24,8},{28,12},{1,17},{... | collective-permute-start | bytes 196616 | tf_op jit(solution)/shard_map/ppermute | solution.py:255
  31.8 3.5 %fusion.4.do_ref = bf16[1024,512]{1,0:T(8,128)(2,1)} fusion(bf16[512,1024]{1,0:T(8,128)(2,1)} %param.11, bf16[1,1024,1024]{2,1,0:T(8,128)(2,1)S(1)} %copy-done), kind=kOutput, calls=%fused_computation.7 | convolution fusion | flops 1074266112 | bytes 4194304 | tf_op jit(solution)/shard_map/dot_general | solution.py:28
  35.3 25.0 %shard_map.121 = (bf16[1024,512]{1,0:T(8,128)(2,1)S(1)}, bf16[1024,512]{1,0:T(8,128)(2,1)S(1)}, f32[1024,512]{1,0:T(8,128)}, f32[1024,512]{1,0:T(8,128)}, f32[2,48,512]{2,1,0:T(8,128)S(1)}) custom-call(bf16[1024,512]{1,0:T(8,128)(2,1)S(1)} %copy-done.4, bf16[1024,512]{1,0:T(8,128)(2,1)S(1)} %get-tuple-element.18.k_ref, bf16[1024,512]{1,0:T(8,128)(2,1)S(1)} %copy-done.6, ...), custom_call_target="tpu_custom_call" | custom-call | tf_op jit(solution)/shard_map/pallas_call | solution.py:211
  60.3 1.0 copy-done.7
  61.3 1.0 copy-done.8
  62.3 2.6 fusion
  64.9 4.1 %convolution_convert_fusion.1 = bf16[1024,1024]{1,0:T(8,128)(2,1)} fusion(bf16[1024,512]{1,0:T(8,128)(2,1)} %copy-done.8, bf16[512,1024]{1,0:T(8,128)(2,1)} %param.11), kind=kOutput, calls=%fused_computation.6 | convolution fusion | flops 1074790400 | bytes 4194304 | tf_op jit(solution)/shard_map/dot_general | solution.py:24
  69.1 0.2 reduce-scatter.7.cloned.1.call-start
  69.3 1.8 collective-permute-start.3
  71.2 3.1 %collective-permute-done.3 = bf16[2,16,512]{2,1,0:T(8,128)(2,1)S(1)} collective-permute-done((bf16[2,16,512]{2,1,0:T(8,128)(2,1)S(1)}, bf16[2,16,512]{2,1,0:T(8,128)(2,1)S(1)}, u32[]{:S(2)}, u32[]{:S(2)}) %collective-permute-start.3) | collective-permute-done | bytes 32800 | tf_op jit(solution)/shard_map/ppermute | solution.py:255
  74.2 0.1 convert_multiply_fusion
  74.3 0.7 broadcast_in_dim.23
  75.0 1.0 reshape.37
  76.0 1.6 collective-permute-start.4
  77.7 4.7 %copy.14 = bf16[1024,3,512]{0,2,1:T(8,128)(2,1)} copy(bf16[1024,3,512]{2,0,1:T(8,128)(2,1)} %param.10) | data formatting | bytes 6291456 | tf_op args[1]
  82.4 0.1 add_multiply_fusion
  82.4 0.7 broadcast_in_dim.24
  83.1 1.0 reshape.38
  84.2 1.6 collective-permute-start.5
  85.8 1.3 constant_dynamic-update-slice_fusion.2
  87.1 1.1 collective-permute-done.5
  88.2 4.7 %shard_map.122 = (bf16[1024,512]{1,0:T(8,128)(2,1)S(1)}, bf16[1024,512]{1,0:T(8,128)(2,1)S(1)}) custom-call(bf16[1024,512]{1,0:T(8,128)(2,1)S(1)} %get-tuple-element.18.k_ref, f32[1024,512]{1,0:T(8,128)S(1)} %copy-done.1, f32[1024,512]{1,0:T(8,128)} %get-tuple-element.25.dk_ref, f32[1024,512]{1,0:T(8,128)} %get-tuple-element.26.dv_ref, ...), custom_call_target="tpu_custom_call" | custom-call | tf_op jit(solution)/shard_map/pallas_call | solution.py:242
  92.9 0.1 constant_dynamic-update-slice_fusion.1
  93.0 1.7 copy-done.10
  94.7 1.3 copy-done.9
  96.0 4.7 %convolution_convert_fusion = bf16[1024,1024]{1,0:T(8,128)(2,1)} fusion(bf16[1024,1536]{1,0:T(8,128)(2,1)S(1)} %constant_dynamic-update-slice_fusion, bf16[1024,1536]{0,1:T(8,128)(2,1)S(1)} %bitcast.34), kind=kOutput, calls=%fused_computation.5 | convolution fusion | flops 3222274048 | bytes 8388608 | tf_op jit(solution)/shard_map/dot_general | solution.py:28
  100.8 6.1 %convolution_bitcast_fusion = f32[192,8,8,128]{3,1,2,0:T(8,128)S(1)} fusion(bf16[1024,1536]{1,0:T(8,128)(2,1)} %copy-done.10, bf16[1,1024,1024]{2,1,0:T(8,128)(2,1)} %param.9), kind=kOutput, calls=%fused_computation | convolution fusion | flops 3221225472 | bytes 11534336 | tf_op jit(solution)/shard_map/dot_general | solution.py:32
  106.8 4.2 %copy.16 = f32[192,8,8,128]{3,2,1,0:T(8,128)} copy(f32[192,8,8,128]{3,1,2,0:T(8,128)S(1)} %convolution_bitcast_fusion) | data formatting | bytes 12582912
  111.0 6.6 %copy.15 = f32[8,2,128,3,256]{4,2,1,0,3:T(8,128)} copy(f32[8,2,128,3,256]{2,0,4,1,3:T(8,128)} %bitcast.32) | data formatting | bytes 12582912 | tf_op jit(solution)/shard_map/transpose | solution.py:310
  117.6 10.0 %reduce-scatter.11.cloned.1.call-done = f32[512,64]{0,1:T(8,128)} async-done(((f32[512,1024]{0,1:T(8,128)}), f32[512,64]{0,1:T(8,128)}) %reduce-scatter.11.cloned.1.call-update) | async-done | bytes 131088 | tf_op jit(solution)/shard_map/reduce_scatter | solution.py:291
  127.6 33.7 %reduce-scatter.5.cloned.1.call-done = bf16[1024,512]{1,0:T(8,128)(2,1)} async-done(((bf16[1024,1024]{1,0:T(8,128)(2,1)}), bf16[1024,512]{1,0:T(8,128)(2,1)}) %reduce-scatter.5.cloned.1.call-update) | async-done | bytes 1048592 | tf_op jit(solution)/shard_map/reduce_scatter | solution.py:289
  161.3 34.7 %reduce-scatter.7.cloned.1.call-done = bf16[1024,512]{1,0:T(8,128)(2,1)} async-done(((bf16[1024,1024]{1,0:T(8,128)(2,1)}), bf16[1024,512]{1,0:T(8,128)(2,1)}) %reduce-scatter.7.cloned.1.call-update) | async-done | bytes 1048592 | tf_op jit(solution)/shard_map/reduce_scatter | solution.py:304
  196.0 90.1 %reduce-scatter.9.cloned.1.call-done = f32[128,3,256]{2,0,1:T(8,128)} async-done(((f32[2048,3,256]{2,0,1:T(8,128)}), f32[128,3,256]{2,0,1:T(8,128)}) %reduce-scatter.9.cloned.1.call-update) | async-done | bytes 393232 | tf_op jit(solution)/shard_map/reduce_scatter | solution.py:311
  (35 shorter events, 0.4 us)
Async XLA Ops:
  7.2 24.7 %copy-start = (bf16[1,1024,1024]{2,1,0:T(8,128)(2,1)S(1)}, bf16[1,1024,1024]{2,1,0:T(8,128)(2,1)}, u32[]{:S(2)}) copy-start(bf16[1,1024,1024]{2,1,0:T(8,128)(2,1)} %param.12) | copy-start | bytes 6291460
  7.2 16.7 %copy-start.11 = (f32[2]{0:T(128)S(1)}, f32[2]{0:T(128)}, u32[]{:S(2)}) copy-start(f32[2]{0:T(128)} %constant.16.clone) | copy-start | bytes 28
  7.2 120.4 %reduce-scatter.11.cloned.1.call-start = ((), (), s32[]{:S(2)}) async-start(), calls=%async_computation.7 | async-start | bytes 2228224 | tf_op jit(solution)/shard_map/reduce_scatter | solution.py:291
  15.1 1.3 copy-start.2
  16.4 1.0 copy-start.3
  17.4 1.0 copy-start.5
  18.4 5.2 %collective-permute-start = (f32[2,16,512]{2,1,0:T(8,128)S(1)}, f32[2,16,512]{2,1,0:T(8,128)S(1)}, u32[]{:S(2)}, u32[]{:S(2)}) collective-permute-start(f32[2,16,512]{2,1,0:T(8,128)S(1)} %get-tuple-element.21), channel_id=1, source_target_pairs={{0,4},{4,0},{8,12},{12,8},{16,20},{20,16},{24,28},{28,24},{1,5},{5... | collective-permute-start | bytes 196616 | tf_op jit(solution)/shard_map/ppermute | solution.py:255
  24.0 4.3 %collective-permute-start.1 = (f32[2,16,512]{2,1,0:T(8,128)S(1)}, f32[2,16,512]{2,1,0:T(8,128)S(1)}, u32[]{:S(2)}, u32[]{:S(2)}) collective-permute-start(f32[2,16,512]{2,1,0:T(8,128)S(1)} %broadcast_multiply_fusion.1), channel_id=1, source_target_pairs={{0,8},{4,12},{8,0},{12,4},{16,24},{20,28},{24,16},{28,20},{1,9},{5... | collective-permute-start | bytes 196616 | tf_op jit(solution)/shard_map/ppermute | solution.py:255
  28.7 6.6 %copy-start.4 = (bf16[1024,512]{1,0:T(8,128)(2,1)S(1)}, bf16[1024,512]{1,0:T(8,128)(2,1)}, u32[]{:S(2)}) copy-start(bf16[1024,512]{1,0:T(8,128)(2,1)} %copy-done.3) | copy-start | bytes 3145732
  28.7 6.6 %copy-start.6 = (bf16[1024,512]{1,0:T(8,128)(2,1)S(1)}, bf16[1024,512]{1,0:T(8,128)(2,1)}, u32[]{:S(2)}) copy-start(bf16[1024,512]{1,0:T(8,128)(2,1)} %copy-done.5) | copy-start | bytes 3145732
  28.7 6.6 %collective-permute-start.2 = (f32[2,16,512]{2,1,0:T(8,128)S(1)}, f32[2,16,512]{2,1,0:T(8,128)S(1)}, u32[]{:S(2)}, u32[]{:S(2)}) collective-permute-start(f32[2,16,512]{2,1,0:T(8,128)S(1)} %broadcast_multiply_fusion), channel_id=1, source_target_pairs={{0,16},{4,20},{8,24},{12,28},{16,0},{20,4},{24,8},{28,12},{1,17},{... | collective-permute-start | bytes 196616 | tf_op jit(solution)/shard_map/ppermute | solution.py:255
  60.3 1.0 copy-start.7
  61.3 1.0 copy-start.8
  64.9 96.4 %reduce-scatter.5.cloned.1.call-start = ((), (), s32[]{:S(2)}) async-start(), calls=%async_computation.4 | async-start | bytes 3145728 | tf_op jit(solution)/shard_map/reduce_scatter | solution.py:289
  69.1 126.9 %reduce-scatter.7.cloned.1.call-start = ((), (), s32[]{:S(2)}) async-start(), calls=%async_computation.5 | async-start | bytes 3145728 | tf_op jit(solution)/shard_map/reduce_scatter | solution.py:304
  69.3 4.9 %collective-permute-start.3 = (bf16[2,16,512]{2,1,0:T(8,128)(2,1)S(1)}, bf16[2,16,512]{2,1,0:T(8,128)(2,1)S(1)}, u32[]{:S(2)}, u32[]{:S(2)}) collective-permute-start(bf16[2,16,512]{2,1,0:T(8,128)(2,1)S(1)} %slice.48), channel_id=1, source_target_pairs={{0,16},{4,20},{8,24},{12,28},{16,0},{20,4},{24,8},{28,12},{1,17},{... | collective-permute-start | bytes 98312 | tf_op jit(solution)/shard_map/ppermute | solution.py:255
  76.0 6.3 %collective-permute-start.4 = (bf16[2,16,512]{2,1,0:T(8,128)(2,1)S(1)}, bf16[2,16,512]{2,1,0:T(8,128)(2,1)S(1)}, u32[]{:S(2)}, u32[]{:S(2)}) collective-permute-start(bf16[2,16,512]{2,1,0:T(8,128)(2,1)S(1)} %add_convert_fusion.1), channel_id=1, source_target_pairs={{0,8},{4,12},{8,0},{12,4},{16,24},{20,28},{24,16},{28,20},{1,9},{5... | collective-permute-start | bytes 98312 | tf_op jit(solution)/shard_map/ppermute | solution.py:255
  84.1 4.0 %copy-start.1 = (f32[1024,512]{1,0:T(8,128)S(1)}, f32[1024,512]{1,0:T(8,128)}, u32[]{:S(2)}) copy-start(f32[1024,512]{1,0:T(8,128)} %get-tuple-element.24.ki_ref) | copy-start | bytes 6291460
  84.2 4.0 %collective-permute-start.5 = (bf16[2,16,512]{2,1,0:T(8,128)(2,1)S(1)}, bf16[2,16,512]{2,1,0:T(8,128)(2,1)S(1)}, u32[]{:S(2)}, u32[]{:S(2)}) collective-permute-start(bf16[2,16,512]{2,1,0:T(8,128)(2,1)S(1)} %add_convert_fusion), channel_id=1, source_target_pairs={{0,4},{4,0},{8,12},{12,8},{16,20},{20,16},{24,28},{28,24},{1,5},{5... | collective-permute-start | bytes 98312 | tf_op jit(solution)/shard_map/ppermute | solution.py:255
  92.9 3.1 %copy-start.9 = (bf16[1024,3,512]{0,2,1:T(8,128)(2,1)S(1)}, bf16[1024,3,512]{0,2,1:T(8,128)(2,1)}, u32[]{:S(2)}) copy-start(bf16[1024,3,512]{0,2,1:T(8,128)(2,1)} %copy.14) | copy-start | bytes 9437188
  93.0 1.7 copy-start.10
  100.7 185.4 %reduce-scatter.9.cloned.1.call-start = ((), (), s32[]{:S(2)}) async-start(), calls=%async_computation.6 | async-start | bytes 6684672 | tf_op jit(solution)/shard_map/reduce_scatter | solution.py:311
Sparse Core Ops, SparseCore 0:
  65.0 62.5 reduce-scatter.10
  130.5 30.7 reduce-scatter.4
  164.1 31.8 reduce-scatter.6
  200.9 85.1 reduce-scatter.8

commit v2 on v1

--- a/solution.py
+++ b/solution.py
@@ -220,33 +220,277 @@
     )(q, k, v, do, qi, far)
 
 
-def finish_kernel(k_ref, ki_ref, dk_ref, dv_ref, far_ref, gk_ref, gv_ref):
-    tokens = k_ref.shape[0]
+def flip(index, group):
+    half = index // group
+    return half + 1 - 2 * (half % 2)
+
+
+def collect_kernel(
+    act_ref, cot_ref, att_ref, merge_ref, w_ref, gq_ref, k_ref, ki_ref, dk_ref, dv_ref, gf_ref,
+    out_ref, gin_ref, gw_ref, gm_ref,
+    far_send, far_recv, gk_ref, gv_ref, xs, xr, w_own, w_ds, w_dr, w_ys, w_yr, w_zs, w_zr,
+    m_own, m_ds, m_dr, m_ys, m_yr, m_zs, m_zr,
+    far_ss, far_rs, x_ss, x_rs, d_ss, d_rs, y_ss, y_rs, z_ss, z_rs,
+):
+    seq, head, dp = lax.axis_index("seq"), lax.axis_index("head"), lax.axis_index("dp")
+    shards = lax.axis_size("seq")
+    bits = shards.bit_length() - 1
+    tokens, model = act_ref.shape
+    cols = att_ref.shape[1]
+    half = model // 2
+    other = 1 - head
+    parity, place = seq % 2, seq // 2
+    places = shards // 2
+    size = model // shards
+    mesh_id = pl.DeviceIdType.MESH
+    barrier = pltpu.get_barrier_semaphore()
+    peers = [(lax.rem(seq + step, shards), head, dp) for step in range(1, shards)]
+    peers += [(seq, other, dp), (seq, head, 1 - dp)]
+    for peer in peers:
+        pl.semaphore_signal(barrier, inc=1, device_id=peer, device_id_type=mesh_id)
+    pl.semaphore_wait(barrier, len(peers))
+
+    def copy(src, dst, send, recv, device):
+        return pltpu.make_async_remote_copy(
+            src_ref=src, dst_ref=dst, send_sem=send, recv_sem=recv,
+            device_id=device, device_id_type=mesh_id,
+        )
+
+    started = []
+    far_waits = []
+    for level in range(bits):
+        group = 1 << level
+        held = gf_ref[:, level * ENTRIES : (level + 1) * ENTRIES, :]
+        held_k = (held[0] * PAIR_FACTORS[0] ** level).astype(BF16)
+        held_v = (held[1] * PAIR_FACTORS[1] ** level).astype(BF16)
+        for i in range(group):
+            slot = group - 1 + i
+            row = lax.broadcasted_iota(jnp.int32, (ENTRIES, ENTRIES), 0)
+            entry = lax.broadcasted_iota(jnp.int32, (ENTRIES, ENTRIES), 1)
+            spread = ((row + ENTRIES * i) // group == entry).astype(BF16)
+            far_send[slot, 0] = dot_nn(spread, held_k).astype(BF16)
+            far_send[slot, 1] = dot_nn(spread, held_v).astype(BF16)
+            there = group - 1 + seq % group
+            peer = (flip(seq, group) * group + i, head, dp)
+            sent = copy(far_send.at[slot], far_recv.at[there], far_ss.at[slot], far_rs.at[there], peer)
+            sent.start()
+            started.append(sent)
+            far_waits.append(
+                copy(far_send.at[slot], far_recv.at[slot], far_ss.at[slot], far_rs.at[slot], peer)
+            )
+
+    chunk = 256
+    chunks = tokens // chunk
+    far_cols = pl.ds(pl.multiple_of(other * half, half), half)
+    own_cols = pl.ds(pl.multiple_of(head * half, half), half)
+
+    def send_x(which, r):
+        at = which * chunks + r
+        sent = copy(xs.at[at], xr.at[at], x_ss.at[at], x_rs.at[at], (seq, other, dp))
+        sent.start()
+        started.append(sent)
+        return sent
+
+    out_copies, in_copies = [], []
+    for r in range(chunks):
+        xs[r] = dot_nn(att_ref[pl.ds(r * chunk, chunk), :], merge_ref[:, far_cols]).astype(BF16)
+        out_copies.append(send_x(0, r))
+
+    def begin_data(c, src, dst):
+        sent = copy(src, dst, d_ss.at[c], d_rs.at[c], (seq, head, 1 - dp))
+        sent.start()
+        started.append(sent)
+        return sent
+
+    data_copies, pair_copies, place_copies = {}, {}, {}
+    first = dp == 0
+    per = max(1, BLOCK // size)
+
+    def merge_term(b, carry):
+        lanes = pl.ds(pl.multiple_of(b * BLOCK, BLOCK), BLOCK)
+        term = dot_tn(cot_ref[:, lanes], att_ref[...])
+        term = term.reshape(per, 2, size // 2, cols)
+        m_own[pl.ds(b * per, per)] = jnp.where(first, term[:, 0], term[:, 1])
+        m_ds[pl.ds(b * per, per)] = jnp.where(first, term[:, 1], term[:, 0]).astype(BF16)
+        return carry
+
+    lax.fori_loop(0, model // BLOCK, merge_term, 0)
+    data_copies[3] = begin_data(3, m_ds, m_dr)
+
+    def weight_stage(c, grads):
+        width = cols // 2
+
+        def body(b, carry):
+            lanes = pl.ds(pl.multiple_of(b * BLOCK, BLOCK), BLOCK)
+            term = dot_tn(act_ref[:, lanes], grads[...])
+            low_part = term[:, :width].reshape(per, size, width)
+            high_part = term[:, width:].reshape(per, size, width)
+            w_own[c, pl.ds(b * per, per)] = jnp.where(first, low_part, high_part)
+            w_ds[c, pl.ds(b * per, per)] = jnp.where(first, high_part, low_part).astype(BF16)
+            return carry
+
+        lax.fori_loop(0, model // BLOCK, body, 0)
+        data_copies[c] = begin_data(c, w_ds.at[c], w_dr.at[c])
+
+    def views(c):
+        if c == 3:
+            return m_own, m_dr, m_ys, m_yr, m_zs, m_zr
+        return tuple(ref.at[c] for ref in (w_own, w_dr, w_ys, w_yr, w_zs, w_zr))
+
+    def pair_stage(c):
+        own, dr, ys, yr, _, _ = views(c)
+        data_copies[c].wait_recv()
+        for i in range(places):
+            s = 2 * i + 1 - parity
+            ys[i] = (own[s] + dr[s].astype(F32)).astype(BF16)
+        sent = copy(ys, yr, y_ss.at[c], y_rs.at[c], (seq + 1 - 2 * parity, head, dp))
+        sent.start()
+        started.append(sent)
+        pair_copies[c] = sent
+
+    def place_stage(c):
+        own, dr, _, yr, zs, zr = views(c)
+        pair_copies[c].wait_recv()
+        for step in range(1, places):
+            target = (place + step) % places
+            s = 2 * target + parity
+            zs[step - 1] = (own[s] + dr[s].astype(F32) + yr[target].astype(F32)).astype(BF16)
+            sent = copy(
+                zs.at[step - 1], zr.at[step - 1], z_ss.at[c, step - 1], z_rs.at[c, step - 1],
+                (s, head, dp),
+            )
+            sent.start()
+            started.append(sent)
+            place_copies[c, step] = sent
+
+    def final_stage(c):
+        own, dr, _, yr, _, zr = views(c)
+        total = own[seq] + dr[seq].astype(F32) + yr[place].astype(F32)
+        for step in range(1, places):
+            place_copies[c, step].wait_recv()
+            total = total + zr[step - 1].astype(F32)
+        if c == 3:
+            gm_ref[...] = total
+        else:
+            gw_ref[c] = total
+
+    for wait in far_waits:
+        wait.wait_recv()
+    carried_k = jnp.zeros((ENTRIES, cols), F32)
+    carried_v = jnp.zeros((ENTRIES, cols), F32)
+    for slot in range(shards - 1):
+        carried_k = carried_k + far_recv[slot, 0].astype(F32)
+        carried_v = carried_v + far_recv[slot, 1].astype(F32)
     window = tokens // ENTRIES
-    far_k = (far_ref[0] * (1.0 / window)).astype(BF16)
-    far_v = (far_ref[1] * (1.0 / math.sqrt(window))).astype(BF16)
-    chunk = min(256, tokens)
+    carried_k = (carried_k * (1.0 / window)).astype(BF16)
+    carried_v = (carried_v * (1.0 / math.sqrt(window))).astype(BF16)
     low = low_half(chunk)
-    for start in range(0, tokens, chunk):
-        rows = pl.ds(start, chunk)
-        spread = spread_matrix(chunk, window, start)
-        g = dk_ref[rows, :] + dot_nn(spread, far_k)
-        u = k_ref[rows, :].astype(F32)
-        gk_ref[rows, :] = (ki_ref[rows, :] * (g - u * half_means(g * u, low))).astype(BF16)
-        gv_ref[rows, :] = (dv_ref[rows, :] + dot_nn(spread, far_v)).astype(BF16)
-
-
-def finish(k, ki, dk, dv, far):
-    tokens, cols = k.shape
-    col = pl.BlockSpec((tokens, LANES), lambda i: (0, i))
+    for r in range(chunks):
+        rows = pl.ds(r * chunk, chunk)
+        spread = spread_matrix(chunk, window, r * chunk)
+        for at in range(0, cols, LANES):
+            lanes = slice(at, at + LANES)
+            g = dk_ref[rows, lanes] + dot_nn(spread, carried_k[:, lanes])
+            u = k_ref[rows, lanes].astype(F32)
+            inv = ki_ref[rows, lanes]
+            gk_ref[rows, lanes] = (inv * (g - u * half_means(g * u, low))).astype(BF16)
+            gv_ref[rows, lanes] = (
+                dv_ref[rows, lanes] + dot_nn(spread, carried_v[:, lanes])
+            ).astype(BF16)
+        total = dot_nt(gq_ref[rows, :], w_ref[0, far_cols, :])
+        total = total + dot_nt(gk_ref[rows, :], w_ref[1, far_cols, :])
+        total = total + dot_nt(gv_ref[rows, :], w_ref[2, far_cols, :])
+        xs[chunks + r] = total.astype(BF16)
+        in_copies.append(send_x(1, r))
+        if r == 0:
+            pair_stage(3)
+
+    def finish_out(r):
+        rows = pl.ds(r * chunk, chunk)
+        total = dot_nn(att_ref[rows, :], merge_ref[:, own_cols])
+        out_copies[r].wait_recv()
+        out_ref[rows, :] = (total + xr[r].astype(F32)).astype(BF16)
+
+    def finish_in(r):
+        rows = pl.ds(r * chunk, chunk)
+        total = dot_nt(gq_ref[rows, :], w_ref[0, own_cols, :])
+        total = total + dot_nt(gk_ref[rows, :], w_ref[1, own_cols, :])
+        total = total + dot_nt(gv_ref[rows, :], w_ref[2, own_cols, :])
+        in_copies[r].wait_recv()
+        gin_ref[rows, :] = (total + xr[chunks + r].astype(F32)).astype(BF16)
+
+    weight_stage(0, gq_ref)
+    place_stage(3)
+    weight_stage(1, gk_ref)
+    pair_stage(0)
+    weight_stage(2, gv_ref)
+    pair_stage(1)
+    place_stage(0)
+    final_stage(3)
+    pair_stage(2)
+    place_stage(1)
+    for r in range(chunks):
+        finish_out(r)
+    place_stage(2)
+    final_stage(0)
+    final_stage(1)
+    final_stage(2)
+    for r in range(chunks):
+        finish_in(r)
+    for sent in started:
+        sent.wait_send()
+
+
+def collect(act, cot, att, merge, weight, gq, k, ki, dk, dv, gf, shards):
+    tokens, model = act.shape
+    cols = att.shape[1]
+    size = model // shards
+    places = shards // 2
+    others = max(1, places - 1)
+    chunks = 2 * (tokens // 256)
+    width = cols // 2
+    vmem = pl.BlockSpec(memory_space=pltpu.VMEM)
+    dma = pltpu.SemaphoreType.DMA
+
+    def stages(lead, rows, lanes):
+        return [
+            pltpu.VMEM(lead + (shards, rows, lanes), F32),
+            pltpu.VMEM(lead + (shards, rows, lanes), BF16),
+            pltpu.VMEM(lead + (shards, rows, lanes), BF16),
+            pltpu.VMEM(lead + (places, rows, lanes), BF16),
+            pltpu.VMEM(lead + (places, rows, lanes), BF16),
+            pltpu.VMEM(lead + (others, rows, lanes), BF16),
+            pltpu.VMEM(lead + (others, rows, lanes), BF16),
+        ]
+
     return pl.pallas_call(
-        finish_kernel,
-        grid=(cols // LANES,),
-        in_specs=[col] * 4 + [pl.BlockSpec((2, ENTRIES, LANES), lambda i: (0, 0, i))],
-        out_specs=[col] * 2,
-        out_shape=[jax.ShapeDtypeStruct((tokens, cols), BF16)] * 2,
-        compiler_params=pltpu.CompilerParams(vmem_limit_bytes=VMEM_LIMIT),
-    )(k, ki, dk, dv, far)
+        collect_kernel,
+        in_specs=[vmem] * 11,
+        out_specs=[vmem] * 4,
+        out_shape=[
+            jax.ShapeDtypeStruct((tokens, model // 2), BF16),
+            jax.ShapeDtypeStruct((tokens, model // 2), BF16),
+            jax.ShapeDtypeStruct((3, size, width), F32),
+            jax.ShapeDtypeStruct((size // 2, cols), F32),
+        ],
+        scratch_shapes=[
+            pltpu.VMEM((shards - 1, 2, ENTRIES, cols), BF16),
+            pltpu.VMEM((shards - 1, 2, ENTRIES, cols), BF16),
+            pltpu.VMEM((tokens, cols), BF16),
+            pltpu.VMEM((tokens, cols), BF16),
+            pltpu.VMEM((chunks, 256, model // 2), BF16),
+            pltpu.VMEM((chunks, 256, model // 2), BF16),
+        ]
+        + stages((3,), size, width)
+        + stages((), size // 2, cols)
+        + [
+            dma((shards - 1,)), dma((shards - 1,)), dma((chunks,)), dma((chunks,)),
+            dma((4,)), dma((4,)), dma((4,)), dma((4,)), dma((4, others)), dma((4, others)),
+        ],
+        compiler_params=pltpu.CompilerParams(
+            vmem_limit_bytes=60 * 1024 * 1024, collective_id=1, has_side_effects=True
+        ),
+    )(act, cot, att, merge, weight, gq, k, ki, dk, dv, gf)
 
 
 def partner_2(value, axis, apart):
@@ -285,31 +529,10 @@
             current = pair_stack(jnp.concatenate([lower_half, upper_half], axis=1))
     do = dot_nt(cot, merge_weight).astype(BF16)
     att, gq, dk, dv, grad_far = attend(q, k, v, do, qi, jnp.concatenate(received, axis=1))
-    partial_out = dot_nn(att, merge_weight).astype(BF16)
-    attention_out = lax.psum_scatter(partial_out, "head", scatter_dimension=1, tiled=True)[None]
-    out_term = dot_tn(att, cot)
-    grad_merge = lax.psum_scatter(out_term, ("seq", "dp"), scatter_dimension=1, tiled=True)
-    carried = jnp.zeros_like(own)
-    for level in reversed(range(bit_count)):
-        spread = jnp.repeat(carried * pair_factors(), 2, axis=1)
-        lower_grad, upper_grad = spread[:, :ENTRIES], spread[:, ENTRIES:]
-        own_grad = jnp.where(uppers[level], upper_grad, lower_grad)
-        partner_grad = jnp.where(uppers[level], lower_grad, upper_grad)
-        sent = partner_grad + grad_far[:, level * ENTRIES : (level + 1) * ENTRIES]
-        carried = own_grad + partner_2(sent.astype(BF16), "seq", level)
-    gk, gv = finish(k, ki, dk, dv, carried)
-    grads = jnp.concatenate([gq, gk, gv], axis=1)
-    flat = project_weight.reshape(model, 3 * cols)
-    input_term = dot_nt(grads, flat).astype(BF16)
-    grad_activations = lax.psum_scatter(input_term, "head", scatter_dimension=1, tiled=True)[None]
-    data_count = lax.axis_size("dp")
-    part_cols = cols // data_count
-    shard_count = lax.axis_size("seq")
-    shard_rows = model // shard_count
-    term = dot_tn(act, grads).reshape(shard_count, shard_rows, 3, data_count, part_cols)
-    term = jnp.moveaxis(term, 3, 1).reshape(model * data_count, 3, part_cols)
-    grad_project = lax.psum_scatter(term, ("seq", "dp"), scatter_dimension=0, tiled=True)
-    return (attention_out, grad_activations, grad_project, grad_merge)
+    out, grad_in, grad_w, grad_m = collect(
+        act, cot, att, merge_weight, weight, gq, k, ki, dk, dv, grad_far, lax.axis_size("seq")
+    )
+    return (out[None], grad_in[None], jnp.moveaxis(grad_w, 0, 1), grad_m.T)
 
 
 def solution(mesh):

time: 293 us -> 117 us (0.40)
  waiting for transfers between devices: 177 us -> 4.49 us
  Pallas kernels: 37.5 us -> 89.6 us
  local copies, waits for them, and re-layouts: 28.7 us -> 8.87 us
  matrix products: 21 us -> 4.11 us
  between operations: 14 us -> 0.76 us
  starting transfers between devices: 13.5 us -> 8.1 us
    reduce_scatter x4 -> x0, waiting for transfers between devices: 168 us -> none  [the longest x1 90.1 us: local(): lax.psum_scatter(term, ('seq', 'dp'), scatter_dimension=0, tiled=True)]
    pallas_call x1, Pallas kernels: 4.66 us -> 56.9 us  [collect(): pl.pallas_call(collect_kernel, in_specs=[vmem] * 11, out_specs=[vmem] * 4...]
    dot_general x3 -> x0, matrix products: 12.8 us -> none  [the longest x2 8.66 us: dot_tn(): lax.dot_general(a, b, (((0,), (0,)), ((), ())), preferred_element_type=F32)]
    unnamed x28 -> x22, local copies, waits for them, and re-layouts: 18.4 us -> 8.73 us
    transpose x1 -> x0, local copies, waits for them, and re-layouts: 6.59 us -> none  [local(): term = jnp.moveaxis(term, 3, 1).reshape(model * data_count, 3, part_cols)]
    ppermute x6 -> x3, starting transfers between devices: 13.2 us -> 8.1 us  [partner_2(): return lax.ppermute(value, axis, pairs)]
    ppermute x6 -> x3, waiting for transfers between devices: 8.65 us -> 4.49 us  [partner_2(): return lax.ppermute(value, axis, pairs)]
    dot_general x2 -> x1, matrix products: 8.19 us -> 4.11 us  [dot_nt(): lax.dot_general(a, b, (((1,), (1,)), ((), ())), preferred_element_type=F32)]
  transfers between devices with their start and end apart: 10 -> 3, of which waited for: 8 -> 2; matrix products, arithmetic and copies ran while one was open for 13% -> 4% of each run, Pallas kernels for 2% -> 0%
where the time goes in v2:
time: 117 us; the launch traced here: 116 us
  Pallas kernels  89.6 us (77%)
  local copies, waits for them, and re-layouts  8.87 us (8%)
  starting transfers between devices  8.1 us (7%)
  waiting for transfers between devices  4.49 us (4%)
  matrix products  4.11 us (4%)
    pallas_call x1, Pallas kernels, collect(): pl.pallas_call(collect_kernel, in_specs=[vmem] * 11, out_specs=[vmem] * 4...  56.9 us
    pallas_call x1, Pallas kernels, attend(): pl.pallas_call(functools.partial(attend_kernel, far_levels), grid=(cols /...  24.9 us
    unnamed x22, local copies, waits for them, and re-layouts  8.73 us
    ppermute x3, starting transfers between devices, partner_2(): return lax.ppermute(value, axis, pairs)  8.1 us
    pallas_call x1, Pallas kernels, project(): pl.pallas_call(project_kernel, grid=(cols // width,), in_specs=[pl.BlockS...  7.75 us
    ppermute x3, waiting for transfers between devices, partner_2(): return lax.ppermute(value, axis, pairs)  4.49 us
    dot_general x1, matrix products, dot_nt(): lax.dot_general(a, b, (((1,), (1,)), ((), ())), preferred_element_type=F32)  4.11 us
  transfers between devices with their start and end apart: 3, of which 2 were waited for; matrix products, arithmetic and copies ran while one was open for 4% of the time, Pallas kernels for 0%

profile of v2, /device:TPU:0, one launch (start us, length us, event | category | flops | bytes accessed | tf_op | source)
XLA Modules:
  0.0 116.5 jit_solution(6857277744413850414)
XLA Ops:
  0.6 0.0 copy-start.8
  0.6 7.7 %shard_map.93 = (bf16[1024,512]{1,0:T(8,128)(2,1)S(1)}, bf16[1024,512]{1,0:T(8,128)(2,1)S(1)}, bf16[1024,512]{1,0:T(8,128)(2,1)S(1)}, f32[1024,512]{1,0:T(8,128)...) custom-call(bf16[1024,1024]{1,0:T(8,128)(2,1)} %bitcast.12, bf16[3,1024,512]{2,1,0:T(8,128)(2,1)} %bitcast.10), custom_call_target="tpu_custom_call" | custom-call | tf_op jit(solution)/shard_map/pallas_call | solution.py:90
  8.4 0.0 copy-start.1
  8.4 1.3 %copy-done.1 = f32[1024,512]{1,0:T(8,128)} copy-done((f32[1024,512]{1,0:T(8,128)}, f32[1024,512]{1,0:T(8,128)S(1)}, u32[]{:S(2)}) %copy-start.1) | copy-done | bytes 2097176
  9.7 0.0 copy-start
  9.7 3.0 %collective-permute-start = (f32[2,16,512]{2,1,0:T(8,128)S(1)}, f32[2,16,512]{2,1,0:T(8,128)S(1)}, u32[]{:S(2)}, u32[]{:S(2)}) collective-permute-start(f32[2,16,512]{2,1,0:T(8,128)S(1)} %get-tuple-element.23), channel_id=1, source_target_pairs={{0,4},{4,0},{8,12},{12,8},{16,20},{20,16},{24,28},{28,24},{1,5},{5... | collective-permute-start | bytes 196616 | tf_op jit(solution)/shard_map/ppermute | solution.py:499
  12.7 2.2 %collective-permute-done = f32[2,16,512]{2,1,0:T(8,128)S(1)} collective-permute-done((f32[2,16,512]{2,1,0:T(8,128)S(1)}, f32[2,16,512]{2,1,0:T(8,128)S(1)}, u32[]{:S(2)}, u32[]{:S(2)}) %collective-permute-start) | collective-permute-done | bytes 65568 | tf_op jit(solution)/shard_map/ppermute | solution.py:499
  15.0 0.1 reshape.16
  15.1 0.2 reduce_sum.18
  15.2 0.0 copy-done.8
  15.2 0.1 broadcast_multiply_fusion.1
  15.3 2.1 %collective-permute-start.1 = (f32[2,16,512]{2,1,0:T(8,128)S(1)}, f32[2,16,512]{2,1,0:T(8,128)S(1)}, u32[]{:S(2)}, u32[]{:S(2)}) collective-permute-start(f32[2,16,512]{2,1,0:T(8,128)S(1)} %broadcast_multiply_fusion.1), channel_id=1, source_target_pairs={{0,8},{4,12},{8,0},{12,4},{16,24},{20,28},{24,16},{28,20},{1,9},{5... | collective-permute-start | bytes 196616 | tf_op jit(solution)/shard_map/ppermute | solution.py:499
  17.4 2.2 %collective-permute-done.1 = f32[2,16,512]{2,1,0:T(8,128)S(1)} collective-permute-done((f32[2,16,512]{2,1,0:T(8,128)S(1)}, f32[2,16,512]{2,1,0:T(8,128)S(1)}, u32[]{:S(2)}, u32[]{:S(2)}) %collective-permute-start.1) | collective-permute-done | bytes 65568 | tf_op jit(solution)/shard_map/ppermute | solution.py:499
  19.6 0.1 broadcast_select_fusion.1
  19.7 0.1 reshape.17
  19.8 0.2 reduce_sum.19
  20.0 0.1 broadcast_multiply_fusion
  20.1 3.0 %collective-permute-start.2 = (f32[2,16,512]{2,1,0:T(8,128)S(1)}, f32[2,16,512]{2,1,0:T(8,128)S(1)}, u32[]{:S(2)}, u32[]{:S(2)}) collective-permute-start(f32[2,16,512]{2,1,0:T(8,128)S(1)} %broadcast_multiply_fusion), channel_id=1, source_target_pairs={{0,16},{4,20},{8,24},{12,28},{16,0},{20,4},{24,8},{28,12},{1,17},{... | collective-permute-start | bytes 196616 | tf_op jit(solution)/shard_map/ppermute | solution.py:499
  23.1 4.1 %convolution_convert_fusion.do_ref = bf16[1024,512]{1,0:T(8,128)(2,1)} fusion(bf16[512,1024]{1,0:T(8,128)(2,1)} %merge_ref.1, bf16[1,1024,1024]{2,1,0:T(8,128)(2,1)} %param.9), kind=kOutput, calls=%fused_computation | convolution fusion | flops 1074266112 | bytes 4194304 | tf_op jit(solution)/shard_map/dot_general | solution.py:28
  27.2 0.0 collective-permute-done.2
  27.2 0.0 copy-done
  27.3 24.9 %shard_map.94 = (bf16[1024,512]{1,0:T(8,128)(2,1)S(1)}, bf16[1024,512]{1,0:T(8,128)(2,1)S(1)}, f32[1024,512]{1,0:T(8,128)}, f32[1024,512]{1,0:T(8,128)}, f32[2,48,512]{2,1,0:T(8,128)S(1)}) custom-call(bf16[1024,512]{1,0:T(8,128)(2,1)S(1)} %get-tuple-element.19.q_ref, bf16[1024,512]{1,0:T(8,128)(2,1)S(1)} %get-tuple-element.20.k_ref, ...), custom_call_target="tpu_custom_call" | custom-call | tf_op jit(solution)/shard_map/pallas_call | solution.py:211
  52.2 0.0 copy-start.2
  52.2 1.0 copy-done.2
  53.1 0.0 copy-start.3
  53.1 1.0 copy-done.3
  54.1 0.0 copy-start.4
  54.1 0.7 copy-done.4
  54.8 56.9 %shard_map.95 = (bf16[1024,512]{1,0:T(8,128)(2,1)}, bf16[1024,512]{1,0:T(8,128)(2,1)}, f32[3,128,256]{2,1,0:T(8,128)}, f32[64,512]{1,0:T(8,128)}) custom-call(bf16[1024,1024]{1,0:T(8,128)(2,1)} %bitcast.13, bf16[1024,1024]{1,0:T(8,128)(2,1)} %bitcast.14, bf16[1024,512]{1,0:T(8,128)(2,1)} %copy-done.2, bf16[512,1024]{1,0:T(8,128)(2,1)} %merge_ref.1, ...), custom_call_target="tpu_custom_call" | custom-call | tf_op jit(solution)/shard_map/pallas_call | solution.py:466
  111.7 0.0 copy-start.5
  111.7 0.0 copy-start.6
  111.7 0.0 copy-start.7
  111.7 2.4 %copy.14 = bf16[1,1024,512]{2,1,0:T(8,128)(2,1)} copy(bf16[1,1024,512]{2,1,0:T(8,128)(2,1)} %bitcast.16) | data formatting | bytes 2097152
  114.1 0.0 copy-done.5
  114.1 1.0 copy.15
  115.1 0.0 copy-done.6
  115.1 0.7 copy.16
  115.8 0.0 copy-done.7
  115.8 0.7 copy.17
  (4 shorter events, 0.0 us)
Async XLA Ops:
  0.6 14.6 %copy-start.8 = (f32[2]{0:T(128)S(1)}, f32[2]{0:T(128)}, u32[]{:S(2)}) copy-start(f32[2]{0:T(128)} %constant.14.clone) | copy-start | bytes 28
  8.4 1.3 %copy-start.1 = (f32[1024,512]{1,0:T(8,128)}, f32[1024,512]{1,0:T(8,128)S(1)}, u32[]{:S(2)}) copy-start(f32[1024,512]{1,0:T(8,128)S(1)} %get-tuple-element.22.qi_ref) | copy-start | bytes 6291460
  9.7 17.5 %copy-start = (bf16[1024,512]{1,0:T(8,128)(2,1)}, bf16[1024,512]{1,0:T(8,128)(2,1)S(1)}, u32[]{:S(2)}) copy-start(bf16[1024,512]{1,0:T(8,128)(2,1)S(1)} %get-tuple-element.20.k_ref) | copy-start | bytes 3145732
  9.7 5.2 %collective-permute-start = (f32[2,16,512]{2,1,0:T(8,128)S(1)}, f32[2,16,512]{2,1,0:T(8,128)S(1)}, u32[]{:S(2)}, u32[]{:S(2)}) collective-permute-start(f32[2,16,512]{2,1,0:T(8,128)S(1)} %get-tuple-element.23), channel_id=1, source_target_pairs={{0,4},{4,0},{8,12},{12,8},{16,20},{20,16},{24,28},{28,24},{1,5},{5... | collective-permute-start | bytes 196616 | tf_op jit(solution)/shard_map/ppermute | solution.py:499
  15.3 4.3 %collective-permute-start.1 = (f32[2,16,512]{2,1,0:T(8,128)S(1)}, f32[2,16,512]{2,1,0:T(8,128)S(1)}, u32[]{:S(2)}, u32[]{:S(2)}) collective-permute-start(f32[2,16,512]{2,1,0:T(8,128)S(1)} %broadcast_multiply_fusion.1), channel_id=1, source_target_pairs={{0,8},{4,12},{8,0},{12,4},{16,24},{20,28},{24,16},{28,20},{1,9},{5... | collective-permute-start | bytes 196616 | tf_op jit(solution)/shard_map/ppermute | solution.py:499
  20.1 7.2 %collective-permute-start.2 = (f32[2,16,512]{2,1,0:T(8,128)S(1)}, f32[2,16,512]{2,1,0:T(8,128)S(1)}, u32[]{:S(2)}, u32[]{:S(2)}) collective-permute-start(f32[2,16,512]{2,1,0:T(8,128)S(1)} %broadcast_multiply_fusion), channel_id=1, source_target_pairs={{0,16},{4,20},{8,24},{12,28},{16,0},{20,4},{24,8},{28,12},{1,17},{... | collective-permute-start | bytes 196616 | tf_op jit(solution)/shard_map/ppermute | solution.py:499
  52.2 1.0 copy-start.2
  53.1 1.0 copy-start.3
  54.1 0.7 copy-start.4
  111.7 2.4 %copy-start.5 = (bf16[1024,512]{1,0:T(8,128)(2,1)S(1)}, bf16[1024,512]{1,0:T(8,128)(2,1)}, u32[]{:S(2)}) copy-start(bf16[1024,512]{1,0:T(8,128)(2,1)} %get-tuple-element.31) | copy-start | bytes 3145732
  111.7 3.4 %copy-start.6 = (f32[3,128,256]{2,1,0:T(8,128)S(1)}, f32[3,128,256]{2,1,0:T(8,128)}, u32[]{:S(2)}) copy-start(f32[3,128,256]{2,1,0:T(8,128)} %get-tuple-element.32) | copy-start | bytes 1179652
  111.7 4.1 %copy-start.7 = (f32[64,512]{1,0:T(8,128)S(1)}, f32[64,512]{1,0:T(8,128)}, u32[]{:S(2)}) copy-start(f32[64,512]{1,0:T(8,128)} %get-tuple-element.33) | copy-start | bytes 393220

commit v3 on v2

--- a/solution.py
+++ b/solution.py
@@ -60,50 +60,8 @@
     return ((token + offset) // window == entry).astype(BF16)
 
 
-def project_kernel(act_ref, w_ref, q_ref, k_ref, v_ref, qi_ref, ki_ref, own_ref):
-    tokens = act_ref.shape[0]
-    width = w_ref.shape[2]
-    chunk = min(256, tokens)
-    low = low_half(chunk)
-    for start in range(0, tokens, chunk):
-        rows = pl.ds(start, chunk)
-        act = act_ref[rows, :]
-        for j, (unit_ref, inv_ref) in enumerate(((q_ref, qi_ref), (k_ref, ki_ref))):
-            raw = dot_nn(act, w_ref[j])
-            for at in range(0, width, LANES):
-                part = raw[:, at : at + LANES]
-                inv = lax.rsqrt(half_means(part * part, low) + EPSILON)
-                unit_ref[rows, at : at + LANES] = (part * inv).astype(BF16)
-                inv_ref[rows, at : at + LANES] = inv
-        v_ref[rows, :] = dot_nn(act, w_ref[2]).astype(BF16)
-    window = tokens // ENTRIES
-    pool = pool_matrix(tokens, window)
-    own_ref[0] = dot_nn(pool, k_ref[...]) * (1.0 / window)
-    own_ref[1] = dot_nn(pool, v_ref[...]) * (1.0 / math.sqrt(window))
-
-
-def project(act, weight):
-    tokens, model = act.shape
-    cols = weight.shape[2]
-    width = 256
-    col = pl.BlockSpec((tokens, width), lambda i: (0, i))
-    return pl.pallas_call(
-        project_kernel,
-        grid=(cols // width,),
-        in_specs=[
-            pl.BlockSpec((tokens, model), lambda i: (0, 0)),
-            pl.BlockSpec((3, model, width), lambda i: (0, 0, i)),
-        ],
-        out_specs=[col] * 5 + [pl.BlockSpec((2, ENTRIES, width), lambda i: (0, 0, i))],
-        out_shape=[jax.ShapeDtypeStruct((tokens, cols), BF16)] * 3
-        + [jax.ShapeDtypeStruct((tokens, cols), F32)] * 2
-        + [jax.ShapeDtypeStruct((2, ENTRIES, cols), F32)],
-        compiler_params=pltpu.CompilerParams(vmem_limit_bytes=VMEM_LIMIT),
-    )(act, weight)
-
-
-def attend_kernel(
-    far_levels, q_ref, k_ref, v_ref, do_ref, qi_ref, far_ref, att_ref, gq_ref, dk_ref, dv_ref, gf_ref
+def attend_pair(
+    far_levels, lanes, q_ref, k_ref, v_ref, do_ref, qi_ref, far_ref, att_ref, gq_ref, dk_ref, dv_ref, gf_ref
 ):
     tokens = q_ref.shape[0]
     blocks = tokens // BLOCK
@@ -118,13 +76,13 @@
         pool = pool_matrix(span, POOL << l)
         pooled_k.append(
             [
-                (dot_nn(pool, k_ref[pl.ds(g * span, span), :]) * key_scale[l])
+                (dot_nn(pool, k_ref[pl.ds(g * span, span), lanes]) * key_scale[l])
                 for g in range(blocks >> l)
             ]
         )
         pooled_v.append(
             [
-                (dot_nn(pool, v_ref[pl.ds(g * span, span), :]) * value_scale[l])
+                (dot_nn(pool, v_ref[pl.ds(g * span, span), lanes]) * value_scale[l])
                 for g in range(blocks >> l)
             ]
         )
@@ -143,16 +101,16 @@
 
     for b in range(blocks):
         rows = pl.ds(b * BLOCK, BLOCK)
-        unit = q_ref[rows, :]
+        unit = q_ref[rows, lanes]
         q = unit * jnp.asarray(0.125, BF16)
-        do = do_ref[rows, :]
+        do = do_ref[rows, lanes]
         kc = jnp.concatenate(
-            [pooled_k[l][(b >> l) ^ 1] for l in range(levels)] + [far_ref[0]] + pad, axis=0
+            [pooled_k[l][(b >> l) ^ 1] for l in range(levels)] + [far_ref[0, :, lanes]] + pad, axis=0
         ).astype(BF16)
         vc = jnp.concatenate(
-            [pooled_v[l][(b >> l) ^ 1] for l in range(levels)] + [far_ref[1]] + pad, axis=0
+            [pooled_v[l][(b >> l) ^ 1] for l in range(levels)] + [far_ref[1, :, lanes]] + pad, axis=0
         ).astype(BF16)
-        kf, vf = k_ref[rows, :], v_ref[rows, :]
+        kf, vf = k_ref[rows, lanes], v_ref[rows, lanes]
         keys = jnp.concatenate([kf * low_b, kf * high_b, kc * low_b, kc * high_b], axis=0)
         values = jnp.concatenate([vf * low_b, vf * high_b, vc * low_b, vc * high_b], axis=0)
         scores = dot_nt(q, keys)
@@ -163,7 +121,7 @@
         p = [e[i] * inv[i % 2] for i in range(4)]
         pb = jnp.concatenate([part.astype(BF16) for part in p], axis=1)
         out = dot_nn(pb, values)
-        att_ref[rows, :] = out.astype(BF16)
+        att_ref[rows, lanes] = out.astype(BF16)
         delta = half_sums(out * do.astype(F32), low)
         dp = dot_nt(do, values)
         ds = jnp.concatenate(
@@ -175,11 +133,11 @@
         )
         dq = dot_nn(ds, keys) * 0.125
         u = unit.astype(F32)
-        gq_ref[rows, :] = (qi_ref[rows, :] * (dq - u * half_means(dq * u, low))).astype(BF16)
+        gq_ref[rows, lanes] = (qi_ref[rows, lanes] * (dq - u * half_means(dq * u, low))).astype(BF16)
         dk = dot_tn(ds, q)
         dv = dot_tn(pb, do)
-        dk_ref[rows, :] = jnp.where(low, dk[0:BLOCK], dk[BLOCK : 2 * BLOCK])
-        dv_ref[rows, :] = jnp.where(low, dv[0:BLOCK], dv[BLOCK : 2 * BLOCK])
+        dk_ref[rows, lanes] = jnp.where(low, dk[0:BLOCK], dk[BLOCK : 2 * BLOCK])
+        dv_ref[rows, lanes] = jnp.where(low, dv[0:BLOCK], dv[BLOCK : 2 * BLOCK])
         dkc = jnp.where(low, dk[2 * BLOCK : 3 * BLOCK], dk[3 * BLOCK :])
         dvc = jnp.where(low, dv[2 * BLOCK : 3 * BLOCK], dv[3 * BLOCK :])
         for l in range(levels):
@@ -188,8 +146,8 @@
             add(grad_v, l, (b >> l) ^ 1, dvc[part])
         far_k = far_k + dkc[levels * ENTRIES : coarse]
         far_v = far_v + dvc[levels * ENTRIES : coarse]
-    gf_ref[0] = far_k
-    gf_ref[1] = far_v
+    gf_ref[0, :, lanes] = far_k
+    gf_ref[1, :, lanes] = far_v
     for b in range(blocks):
         rows = pl.ds(b * BLOCK, BLOCK)
         spread = jnp.concatenate(
@@ -199,25 +157,8 @@
         held_v = [grad_v[l][b >> l] * value_scale[l] for l in range(levels)]
         held_k = jnp.concatenate(held_k, axis=0).astype(BF16)
         held_v = jnp.concatenate(held_v, axis=0).astype(BF16)
-        dk_ref[rows, :] += dot_nn(spread, held_k)
-        dv_ref[rows, :] += dot_nn(spread, held_v)
-
-
-def attend(q, k, v, do, qi, far):
-    tokens, cols = q.shape
-    far_levels = far.shape[1] // ENTRIES
-    col = pl.BlockSpec((tokens, LANES), lambda i: (0, i))
-    few = pl.BlockSpec((2, far_levels * ENTRIES, LANES), lambda i: (0, 0, i))
-    return pl.pallas_call(
-        functools.partial(attend_kernel, far_levels),
-        grid=(cols // LANES,),
-        in_specs=[col] * 5 + [few],
-        out_specs=[col] * 4 + [few],
-        out_shape=[jax.ShapeDtypeStruct((tokens, cols), BF16)] * 2
-        + [jax.ShapeDtypeStruct((tokens, cols), F32)] * 2
-        + [jax.ShapeDtypeStruct(far.shape, F32)],
-        compiler_params=pltpu.CompilerParams(vmem_limit_bytes=VMEM_LIMIT),
-    )(q, k, v, do, qi, far)
+        dk_ref[rows, lanes] += dot_nn(spread, held_k)
+        dv_ref[rows, lanes] += dot_nn(spread, held_v)
 
 
 def flip(index, group):
@@ -225,11 +166,14 @@
     return half + 1 - 2 * (half % 2)
 
 
-def collect_kernel(
-    act_ref, cot_ref, att_ref, merge_ref, w_ref, gq_ref, k_ref, ki_ref, dk_ref, dv_ref, gf_ref,
+def layer_kernel(
+    act_ref, cot_ref, merge_ref, w_ref,
     out_ref, gin_ref, gw_ref, gm_ref,
+    q_ref, k_ref, v_ref, qi_ref, ki_ref, do_ref, att_ref, gq_ref, dk_ref, dv_ref, gf_ref,
+    own_ref, gathered, far_ref, att_other, merge_send, merge_recv,
     far_send, far_recv, gk_ref, gv_ref, xs, xr, w_own, w_ds, w_dr, w_ys, w_yr, w_zs, w_zr,
     m_own, m_ds, m_dr, m_ys, m_yr, m_zs, m_zr,
+    own_ss, own_rs, att_ss, att_rs, merge_sem,
     far_ss, far_rs, x_ss, x_rs, d_ss, d_rs, y_ss, y_rs, z_ss, z_rs,
 ):
     seq, head, dp = lax.axis_index("seq"), lax.axis_index("head"), lax.axis_index("dp")
@@ -248,6 +192,32 @@
     peers += [(seq, other, dp), (seq, head, 1 - dp)]
     for peer in peers:
         pl.semaphore_signal(barrier, inc=1, device_id=peer, device_id_type=mesh_id)
+
+    window = tokens // ENTRIES
+    chunk = 256
+    chunks = tokens // chunk
+    low = low_half(chunk)
+
+    def project_rows(r, carry):
+        rows = pl.ds(pl.multiple_of(r * chunk, chunk), chunk)
+        act = act_ref[rows, :]
+        for at in range(0, cols, 256):
+            wide = slice(at, at + 256)
+            for j, (unit_ref, inv_ref) in enumerate(((q_ref, qi_ref), (k_ref, ki_ref))):
+                raw = dot_nn(act, w_ref[j, :, wide])
+                for part_at in range(0, 256, LANES):
+                    part = raw[:, part_at : part_at + LANES]
+                    inv = lax.rsqrt(half_means(part * part, low) + EPSILON)
+                    lanes = slice(at + part_at, at + part_at + LANES)
+                    unit_ref[rows, lanes] = (part * inv).astype(BF16)
+                    inv_ref[rows, lanes] = inv
+            v_ref[rows, wide] = dot_nn(act, w_ref[2, :, wide]).astype(BF16)
+        return carry
+
+    lax.fori_loop(0, chunks, project_rows, 0)
+    pool = pool_matrix(tokens, window)
+    own_ref[0] = (dot_nn(pool, k_ref[...]) * (1.0 / window)).astype(BF16)
+    own_ref[1] = (dot_nn(pool, v_ref[...]) * (1.0 / math.sqrt(window))).astype(BF16)
     pl.semaphore_wait(barrier, len(peers))
 
     def copy(src, dst, send, recv, device):
@@ -258,6 +228,60 @@
 
     started = []
     far_waits = []
+    far_cols = pl.ds(pl.multiple_of(other * half, half), half)
+    own_cols = pl.ds(pl.multiple_of(head * half, half), half)
+    own_waits = []
+    for step in range(1, shards):
+        peer = (lax.rem(seq + step, shards), head, dp)
+        sent = copy(own_ref, gathered.at[seq], own_ss.at[step - 1], own_rs.at[step - 1], peer)
+        sent.start()
+        started.append(sent)
+        source = lax.rem(seq + shards - step, shards)
+        own_waits.append(
+            copy(own_ref, gathered.at[source], own_ss.at[step - 1], own_rs.at[step - 1], peer)
+        )
+    merge_send[...] = merge_ref[:, far_cols]
+    merge_copy = copy(merge_send, merge_recv, merge_sem.at[0], merge_sem.at[1], (seq, other, dp))
+    merge_copy.start()
+    started.append(merge_copy)
+
+    def attended_back(r, carry):
+        rows = pl.ds(pl.multiple_of(r * chunk, chunk), chunk)
+        do_ref[rows, :] = dot_nt(cot_ref[rows, :], merge_ref[...]).astype(BF16)
+        return carry
+
+    lax.fori_loop(0, chunks, attended_back, 0)
+    for wait in own_waits:
+        wait.wait_recv()
+    for level in range(bits):
+        group = 1 << level
+        held = gathered[pl.ds(flip(seq, group) * group, group)]
+        pool = pool_matrix(group * ENTRIES, group)
+        part = pl.ds(level * ENTRIES, ENTRIES)
+        for kind in range(2):
+            mean = dot_nn(pool, held[:, kind].reshape(group * ENTRIES, cols))
+            far_ref[kind, part, :] = mean * PAIR_FACTORS[kind] ** level
+
+    def att_copy(p):
+        lanes = pl.ds(pl.multiple_of(p * LANES, LANES), LANES)
+        return copy(
+            att_ref.at[:, lanes], att_other.at[:, lanes], att_ss.at[p], att_rs.at[p],
+            (seq, other, dp),
+        )
+
+    def pair_body(p, carry):
+        lanes = pl.ds(pl.multiple_of(p * LANES, LANES), LANES)
+        attend_pair(
+            bits, lanes, q_ref, k_ref, v_ref, do_ref, qi_ref, far_ref,
+            att_ref, gq_ref, dk_ref, dv_ref, gf_ref,
+        )
+        att_copy(p).start()
+        return carry
+
+    pairs = cols // LANES
+    lax.fori_loop(0, pairs, pair_body, 0)
+    for p in range(pairs):
+        started.append(att_copy(p))
     for level in range(bits):
         group = 1 << level
         held = gf_ref[:, level * ENTRIES : (level + 1) * ENTRIES, :]
@@ -279,22 +303,13 @@
                 copy(far_send.at[slot], far_recv.at[slot], far_ss.at[slot], far_rs.at[slot], peer)
             )
 
-    chunk = 256
-    chunks = tokens // chunk
-    far_cols = pl.ds(pl.multiple_of(other * half, half), half)
-    own_cols = pl.ds(pl.multiple_of(head * half, half), half)
-
-    def send_x(which, r):
-        at = which * chunks + r
+    def send_x(at):
         sent = copy(xs.at[at], xr.at[at], x_ss.at[at], x_rs.at[at], (seq, other, dp))
         sent.start()
         started.append(sent)
         return sent
 
-    out_copies, in_copies = [], []
-    for r in range(chunks):
-        xs[r] = dot_nn(att_ref[pl.ds(r * chunk, chunk), :], merge_ref[:, far_cols]).astype(BF16)
-        out_copies.append(send_x(0, r))
+    in_copies = []
 
     def begin_data(c, src, dst):
         sent = copy(src, dst, d_ss.at[c], d_rs.at[c], (seq, head, 1 - dp))
@@ -381,10 +396,8 @@
     for slot in range(shards - 1):
         carried_k = carried_k + far_recv[slot, 0].astype(F32)
         carried_v = carried_v + far_recv[slot, 1].astype(F32)
-    window = tokens // ENTRIES
     carried_k = (carried_k * (1.0 / window)).astype(BF16)
     carried_v = (carried_v * (1.0 / math.sqrt(window))).astype(BF16)
-    low = low_half(chunk)
     for r in range(chunks):
         rows = pl.ds(r * chunk, chunk)
         spread = spread_matrix(chunk, window, r * chunk)
@@ -400,16 +413,16 @@
         total = dot_nt(gq_ref[rows, :], w_ref[0, far_cols, :])
         total = total + dot_nt(gk_ref[rows, :], w_ref[1, far_cols, :])
         total = total + dot_nt(gv_ref[rows, :], w_ref[2, far_cols, :])
-        xs[chunks + r] = total.astype(BF16)
-        in_copies.append(send_x(1, r))
+        xs[r] = total.astype(BF16)
+        in_copies.append(send_x(r))
         if r == 0:
             pair_stage(3)
 
     def finish_out(r):
         rows = pl.ds(r * chunk, chunk)
         total = dot_nn(att_ref[rows, :], merge_ref[:, own_cols])
-        out_copies[r].wait_recv()
-        out_ref[rows, :] = (total + xr[r].astype(F32)).astype(BF16)
+        total = total + dot_nn(att_other[rows, :], merge_recv[...])
+        out_ref[rows, :] = total.astype(BF16)
 
     def finish_in(r):
         rows = pl.ds(r * chunk, chunk)
@@ -417,7 +430,7 @@
         total = total + dot_nt(gk_ref[rows, :], w_ref[1, own_cols, :])
         total = total + dot_nt(gv_ref[rows, :], w_ref[2, own_cols, :])
         in_copies[r].wait_recv()
-        gin_ref[rows, :] = (total + xr[chunks + r].astype(F32)).astype(BF16)
+        gin_ref[rows, :] = (total + xr[r].astype(F32)).astype(BF16)
 
     weight_stage(0, gq_ref)
     place_stage(3)
@@ -429,6 +442,9 @@
     final_stage(3)
     pair_stage(2)
     place_stage(1)
+    merge_copy.wait_recv()
+    for p in range(pairs):
+        att_copy(p).wait_recv()
     for r in range(chunks):
         finish_out(r)
     place_stage(2)
@@ -441,13 +457,16 @@
         sent.wait_send()
 
 
-def collect(act, cot, att, merge, weight, gq, k, ki, dk, dv, gf, shards):
+def layer(act, cot, merge, weight, shards):
     tokens, model = act.shape
-    cols = att.shape[1]
+    cols = merge.shape[0]
+    far_rows = (shards.bit_length() - 1) * ENTRIES
+    pairs = cols // LANES
+    full, wide = pltpu.VMEM((tokens, cols), BF16), pltpu.VMEM((tokens, cols), F32)
     size = model // shards
     places = shards // 2
     others = max(1, places - 1)
-    chunks = 2 * (tokens // 256)
+    chunks = tokens // 256
     width = cols // 2
     vmem = pl.BlockSpec(memory_space=pltpu.VMEM)
     dma = pltpu.SemaphoreType.DMA
@@ -464,8 +483,8 @@
         ]
 
     return pl.pallas_call(
-        collect_kernel,
-        in_specs=[vmem] * 11,
+        layer_kernel,
+        in_specs=[vmem] * 4,
         out_specs=[vmem] * 4,
         out_shape=[
             jax.ShapeDtypeStruct((tokens, model // 2), BF16),
@@ -473,7 +492,15 @@
             jax.ShapeDtypeStruct((3, size, width), F32),
             jax.ShapeDtypeStruct((size // 2, cols), F32),
         ],
-        scratch_shapes=[
+        scratch_shapes=[full] * 3 + [wide] * 2 + [full] * 3 + [wide] * 2
+        + [
+            pltpu.VMEM((2, far_rows, cols), F32),
+            pltpu.VMEM((2, ENTRIES, cols), BF16),
+            pltpu.VMEM((shards, 2, ENTRIES, cols), BF16),
+            pltpu.VMEM((2, far_rows, cols), F32),
+            full,
+            pltpu.VMEM((cols, model // 2), BF16),
+            pltpu.VMEM((cols, model // 2), BF16),
             pltpu.VMEM((shards - 1, 2, ENTRIES, cols), BF16),
             pltpu.VMEM((shards - 1, 2, ENTRIES, cols), BF16),
             pltpu.VMEM((tokens, cols), BF16),
@@ -484,53 +511,20 @@
         + stages((3,), size, width)
         + stages((), size // 2, cols)
         + [
+            dma((shards - 1,)), dma((shards - 1,)), dma((pairs,)), dma((pairs,)), dma((2,)),
             dma((shards - 1,)), dma((shards - 1,)), dma((chunks,)), dma((chunks,)),
             dma((4,)), dma((4,)), dma((4,)), dma((4,)), dma((4, others)), dma((4, others)),
         ],
         compiler_params=pltpu.CompilerParams(
             vmem_limit_bytes=60 * 1024 * 1024, collective_id=1, has_side_effects=True
         ),
-    )(act, cot, att, merge, weight, gq, k, ki, dk, dv, gf)
-
-
-def partner_2(value, axis, apart):
-    mask = 2**apart
-    pairs = [(source, source ^ mask) for source in range(lax.axis_size(axis))]
-    return lax.ppermute(value, axis, pairs)
-
-
-def pair_factors():
-    return jnp.array(PAIR_FACTORS, F32)[:, None, None]
-
-
-def pair_stack(stacked):
-    half_count = stacked.shape[1] // 2
-    return stacked.reshape(2, half_count, 2, stacked.shape[2]).sum(axis=2) * pair_factors()
+    )(act, cot, merge, weight)
 
 
 def local(activations, project_weight, merge_weight, cotangent):
-    act = activations[0]
-    cot = cotangent[0]
-    tokens, model = act.shape
-    cols = project_weight.shape[2]
     weight = jnp.moveaxis(project_weight, 1, 0)
-    q, k, v, qi, ki, own = project(act, weight)
-    bit_count = lax.axis_size("seq").bit_length() - 1
-    seq_index = lax.axis_index("seq")
-    uppers = [seq_index >> level & 1 == 1 for level in range(bit_count)]
-    received = []
-    current = own
-    for level in range(bit_count):
-        partner = partner_2(current, "seq", level)
-        received.append(partner)
-        if level + 1 < bit_count:
-            lower_half = jnp.where(uppers[level], partner, current)
-            upper_half = jnp.where(uppers[level], current, partner)
-            current = pair_stack(jnp.concatenate([lower_half, upper_half], axis=1))
-    do = dot_nt(cot, merge_weight).astype(BF16)
-    att, gq, dk, dv, grad_far = attend(q, k, v, do, qi, jnp.concatenate(received, axis=1))
-    out, grad_in, grad_w, grad_m = collect(
-        act, cot, att, merge_weight, weight, gq, k, ki, dk, dv, grad_far, lax.axis_size("seq")
+    out, grad_in, grad_w, grad_m = layer(
+        activations[0], cotangent[0], merge_weight, weight, lax.axis_size("seq")
     )
     return (out[None], grad_in[None], jnp.moveaxis(grad_w, 0, 1), grad_m.T)
 

time: 117 us -> 91.6 us (0.78)
  starting transfers between devices: 8.1 us -> 0 us
  waiting for transfers between devices: 4.49 us -> 0 us
  matrix products: 4.11 us -> 0 us
  local copies, waits for them, and re-layouts: 8.87 us -> 4.76 us
  Pallas kernels: 89.6 us -> 86 us
    ppermute x3 -> x0, starting transfers between devices: 8.1 us -> none  [partner_2(): return lax.ppermute(value, axis, pairs)]
    ppermute x3 -> x0, waiting for transfers between devices: 4.49 us -> none  [partner_2(): return lax.ppermute(value, axis, pairs)]
    dot_general x1 -> x0, matrix products: 4.11 us -> none  [dot_nt(): lax.dot_general(a, b, (((1,), (1,)), ((), ())), preferred_element_type=F32)]
    unnamed x22 -> x10, local copies, waits for them, and re-layouts: 8.73 us -> 4.76 us
    pallas_call x3 -> x1, Pallas kernels: 89.6 us -> 86 us  [layer(): pl.pallas_call(layer_kernel, in_specs=[vmem] * 4, out_specs=[vmem] * 4, o...]
  transfers between devices with their start and end apart: 3 -> 0, of which waited for: 2 -> 0; matrix products, arithmetic and copies ran while one was open for 4% -> 0% of each run, Pallas kernels for 0% -> 0%
where the time goes in v3:
time: 91.6 us; the launch traced here: 91.4 us
  Pallas kernels  86 us (94%)
  local copies, waits for them, and re-layouts  4.76 us (5%)
    pallas_call x1, Pallas kernels, layer(): pl.pallas_call(layer_kernel, in_specs=[vmem] * 4, out_specs=[vmem] * 4, o...  86 us
    unnamed x10, local copies, waits for them, and re-layouts  4.76 us

profile of v3, /device:TPU:0, one launch (start us, length us, event | category | flops | bytes accessed | tf_op | source)
XLA Modules:
  0.0 91.4 jit_solution(901356687622341667)
XLA Ops:
  0.6 86.0 %shard_map.75 = (bf16[1024,512]{1,0:T(8,128)(2,1)}, bf16[1024,512]{1,0:T(8,128)(2,1)}, f32[3,128,256]{2,1,0:T(8,128)}, f32[64,512]{1,0:T(8,128)}) custom-call(bf16[1024,1024]{1,0:T(8,128)(2,1)} %bitcast.8, bf16[1024,1024]{1,0:T(8,128)(2,1)} %bitcast.9, bf16[512,1024]{1,0:T(8,128)(2,1)} %merge_ref.1, bf16[3,1024,512]{2,1,0:T(8,128)(2,1)} %bitcast.7), custom_call_target="tpu_custom_call" | custom-call | tf_op jit(solution)/shard_map/pallas_call | solution.py:485
  86.6 0.0 copy-start
  86.7 0.0 copy-start.1
  86.7 0.0 copy-start.2
  86.7 2.4 %copy.12 = bf16[1,1024,512]{2,1,0:T(8,128)(2,1)} copy(bf16[1,1024,512]{2,1,0:T(8,128)(2,1)} %bitcast.11) | data formatting | bytes 2097152
  89.0 0.0 copy-done
  89.0 1.0 %copy.13 = bf16[1,1024,512]{2,1,0:T(8,128)(2,1)} copy(bf16[1,1024,512]{2,1,0:T(8,128)(2,1)S(1)} %bitcast.10) | data formatting | bytes 2097152
  90.0 0.0 copy-done.1
  90.0 0.7 copy.14
  90.8 0.0 copy-done.2
  90.8 0.7 copy.15
Async XLA Ops:
  86.6 2.4 %copy-start = (bf16[1024,512]{1,0:T(8,128)(2,1)S(1)}, bf16[1024,512]{1,0:T(8,128)(2,1)}, u32[]{:S(2)}) copy-start(bf16[1024,512]{1,0:T(8,128)(2,1)} %get-tuple-element.9) | copy-start | bytes 3145732
  86.7 3.4 %copy-start.1 = (f32[3,128,256]{2,1,0:T(8,128)S(1)}, f32[3,128,256]{2,1,0:T(8,128)}, u32[]{:S(2)}) copy-start(f32[3,128,256]{2,1,0:T(8,128)} %get-tuple-element.10) | copy-start | bytes 1179652
  86.7 4.1 %copy-start.2 = (f32[64,512]{1,0:T(8,128)S(1)}, f32[64,512]{1,0:T(8,128)}, u32[]{:S(2)}) copy-start(f32[64,512]{1,0:T(8,128)} %get-tuple-element.11) | copy-start | bytes 393220

commit v4 on v3

--- a/solution.py
+++ b/solution.py
@@ -262,6 +262,89 @@
             mean = dot_nn(pool, held[:, kind].reshape(group * ENTRIES, cols))
             far_ref[kind, part, :] = mean * PAIR_FACTORS[kind] ** level
 
+    def begin_data(c, src, dst):
+        sent = copy(src, dst, d_ss.at[c], d_rs.at[c], (seq, head, 1 - dp))
+        sent.start()
+        started.append(sent)
+        return sent
+
+    data_copies, pair_copies, place_copies = {}, {}, {}
+    first = dp == 0
+    per = max(1, BLOCK // size)
+
+    def merge_stage(part):
+        width = cols // 2
+        at = slice(part * width, (part + 1) * width)
+
+        def body(b, carry):
+            lanes = pl.ds(pl.multiple_of(b * BLOCK, BLOCK), BLOCK)
+            term = dot_tn(cot_ref[:, lanes], att_ref[:, at])
+            term = term.reshape(per, 2, size // 2, width)
+            here = pl.ds(b * per, per)
+            m_own[part, here] = jnp.where(first, term[:, 0], term[:, 1])
+            m_ds[part, here] = jnp.where(first, term[:, 1], term[:, 0]).astype(BF16)
+            return carry
+
+        lax.fori_loop(0, model // BLOCK, body, 0)
+        data_copies[3 + part] = begin_data(3 + part, m_ds.at[part], m_dr.at[part])
+
+    def weight_stage(c, grads):
+        width = cols // 2
+
+        def body(b, carry):
+            lanes = pl.ds(pl.multiple_of(b * BLOCK, BLOCK), BLOCK)
+            term = dot_tn(act_ref[:, lanes], grads[...])
+            low_part = term[:, :width].reshape(per, size, width)
+            high_part = term[:, width:].reshape(per, size, width)
+            w_own[c, pl.ds(b * per, per)] = jnp.where(first, low_part, high_part)
+            w_ds[c, pl.ds(b * per, per)] = jnp.where(first, high_part, low_part).astype(BF16)
+            return carry
+
+        lax.fori_loop(0, model // BLOCK, body, 0)
+        data_copies[c] = begin_data(c, w_ds.at[c], w_dr.at[c])
+
+    def views(c):
+        if c >= 3:
+            return tuple(ref.at[c - 3] for ref in (m_own, m_dr, m_ys, m_yr, m_zs, m_zr))
+        return tuple(ref.at[c] for ref in (w_own, w_dr, w_ys, w_yr, w_zs, w_zr))
+
+    def pair_stage(c):
+        own, dr, ys, yr, _, _ = views(c)
+        data_copies[c].wait_recv()
+        for i in range(places):
+            s = 2 * i + 1 - parity
+            ys[i] = (own[s] + dr[s].astype(F32)).astype(BF16)
+        sent = copy(ys, yr, y_ss.at[c], y_rs.at[c], (seq + 1 - 2 * parity, head, dp))
+        sent.start()
+        started.append(sent)
+        pair_copies[c] = sent
+
+    def place_stage(c):
+        own, dr, _, yr, zs, zr = views(c)
+        pair_copies[c].wait_recv()
+        for step in range(1, places):
+            target = (place + step) % places
+            s = 2 * target + parity
+            zs[step - 1] = (own[s] + dr[s].astype(F32) + yr[target].astype(F32)).astype(BF16)
+            sent = copy(
+                zs.at[step - 1], zr.at[step - 1], z_ss.at[c, step - 1], z_rs.at[c, step - 1],
+                (s, head, dp),
+            )
+            sent.start()
+            started.append(sent)
+            place_copies[c, step] = sent
+
+    def final_stage(c):
+        own, dr, _, yr, _, zr = views(c)
+        total = own[seq] + dr[seq].astype(F32) + yr[place].astype(F32)
+        for step in range(1, places):
+            place_copies[c, step].wait_recv()
+            total = total + zr[step - 1].astype(F32)
+        if c >= 3:
+            gm_ref[:, (c - 3) * (cols // 2) : (c - 2) * (cols // 2)] = total
+        else:
+            gw_ref[c] = total
+
     def att_copy(p):
         lanes = pl.ds(pl.multiple_of(p * LANES, LANES), LANES)
         return copy(
@@ -279,7 +362,12 @@
         return carry
 
     pairs = cols // LANES
-    lax.fori_loop(0, pairs, pair_body, 0)
+    middle = pairs // 2
+    lax.fori_loop(0, middle, pair_body, 0)
+    merge_stage(0)
+    lax.fori_loop(middle, pairs - 1, pair_body, 0)
+    pair_stage(3)
+    lax.fori_loop(pairs - 1, pairs, pair_body, 0)
     for p in range(pairs):
         started.append(att_copy(p))
     for level in range(bits):
@@ -311,84 +399,10 @@
 
     in_copies = []
 
-    def begin_data(c, src, dst):
-        sent = copy(src, dst, d_ss.at[c], d_rs.at[c], (seq, head, 1 - dp))
-        sent.start()
-        started.append(sent)
-        return sent
-
-    data_copies, pair_copies, place_copies = {}, {}, {}
-    first = dp == 0
-    per = max(1, BLOCK // size)
-
-    def merge_term(b, carry):
-        lanes = pl.ds(pl.multiple_of(b * BLOCK, BLOCK), BLOCK)
-        term = dot_tn(cot_ref[:, lanes], att_ref[...])
-        term = term.reshape(per, 2, size // 2, cols)
-        m_own[pl.ds(b * per, per)] = jnp.where(first, term[:, 0], term[:, 1])
-        m_ds[pl.ds(b * per, per)] = jnp.where(first, term[:, 1], term[:, 0]).astype(BF16)
-        return carry
-
-    lax.fori_loop(0, model // BLOCK, merge_term, 0)
-    data_copies[3] = begin_data(3, m_ds, m_dr)
-
-    def weight_stage(c, grads):
-        width = cols // 2
-
-        def body(b, carry):
-            lanes = pl.ds(pl.multiple_of(b * BLOCK, BLOCK), BLOCK)
-            term = dot_tn(act_ref[:, lanes], grads[...])
-            low_part = term[:, :width].reshape(per, size, width)
-            high_part = term[:, width:].reshape(per, size, width)
-            w_own[c, pl.ds(b * per, per)] = jnp.where(first, low_part, high_part)
-            w_ds[c, pl.ds(b * per, per)] = jnp.where(first, high_part, low_part).astype(BF16)
-            return carry
-
-        lax.fori_loop(0, model // BLOCK, body, 0)
-        data_copies[c] = begin_data(c, w_ds.at[c], w_dr.at[c])
-
-    def views(c):
-        if c == 3:
-            return m_own, m_dr, m_ys, m_yr, m_zs, m_zr
-        return tuple(ref.at[c] for ref in (w_own, w_dr, w_ys, w_yr, w_zs, w_zr))
-
-    def pair_stage(c):
-        own, dr, ys, yr, _, _ = views(c)
-        data_copies[c].wait_recv()
-        for i in range(places):
-            s = 2 * i + 1 - parity
-            ys[i] = (own[s] + dr[s].astype(F32)).astype(BF16)
-        sent = copy(ys, yr, y_ss.at[c], y_rs.at[c], (seq + 1 - 2 * parity, head, dp))
-        sent.start()
-        started.append(sent)
-        pair_copies[c] = sent
-
-    def place_stage(c):
-        own, dr, _, yr, zs, zr = views(c)
-        pair_copies[c].wait_recv()
-        for step in range(1, places):
-            target = (place + step) % places
-            s = 2 * target + parity
-            zs[step - 1] = (own[s] + dr[s].astype(F32) + yr[target].astype(F32)).astype(BF16)
-            sent = copy(
-                zs.at[step - 1], zr.at[step - 1], z_ss.at[c, step - 1], z_rs.at[c, step - 1],
-                (s, head, dp),
-            )
-            sent.start()
-            started.append(sent)
-            place_copies[c, step] = sent
-
-    def final_stage(c):
-        own, dr, _, yr, _, zr = views(c)
-        total = own[seq] + dr[seq].astype(F32) + yr[place].astype(F32)
-        for step in range(1, places):
-            place_copies[c, step].wait_recv()
-            total = total + zr[step - 1].astype(F32)
-        if c == 3:
-            gm_ref[...] = total
-        else:
-            gw_ref[c] = total
-
+    merge_stage(1)
+    place_stage(3)
+    weight_stage(0, gq_ref)
+    pair_stage(4)
     for wait in far_waits:
         wait.wait_recv()
     carried_k = jnp.zeros((ENTRIES, cols), F32)
@@ -416,7 +430,9 @@
         xs[r] = total.astype(BF16)
         in_copies.append(send_x(r))
         if r == 0:
-            pair_stage(3)
+            pair_stage(0)
+        if r == 1:
+            place_stage(4)
 
     def finish_out(r):
         rows = pl.ds(r * chunk, chunk)
@@ -432,27 +448,25 @@
         in_copies[r].wait_recv()
         gin_ref[rows, :] = (total + xr[r].astype(F32)).astype(BF16)
 
-    weight_stage(0, gq_ref)
-    place_stage(3)
     weight_stage(1, gk_ref)
-    pair_stage(0)
-    weight_stage(2, gv_ref)
     pair_stage(1)
     place_stage(0)
+    weight_stage(2, gv_ref)
+    pair_stage(2)
     final_stage(3)
-    pair_stage(2)
-    place_stage(1)
+    final_stage(4)
     merge_copy.wait_recv()
     for p in range(pairs):
         att_copy(p).wait_recv()
     for r in range(chunks):
         finish_out(r)
+    place_stage(1)
+    final_stage(0)
     place_stage(2)
-    final_stage(0)
     final_stage(1)
-    final_stage(2)
     for r in range(chunks):
         finish_in(r)
+    final_stage(2)
     for sent in started:
         sent.wait_send()
 
@@ -509,11 +523,11 @@
             pltpu.VMEM((chunks, 256, model // 2), BF16),
         ]
         + stages((3,), size, width)
-        + stages((), size // 2, cols)
+        + stages((2,), size // 2, width)
         + [
             dma((shards - 1,)), dma((shards - 1,)), dma((pairs,)), dma((pairs,)), dma((2,)),
             dma((shards - 1,)), dma((shards - 1,)), dma((chunks,)), dma((chunks,)),
-            dma((4,)), dma((4,)), dma((4,)), dma((4,)), dma((4, others)), dma((4, others)),
+            dma((5,)), dma((5,)), dma((5,)), dma((5,)), dma((5, others)), dma((5, others)),
         ],
         compiler_params=pltpu.CompilerParams(
             vmem_limit_bytes=60 * 1024 * 1024, collective_id=1, has_side_effects=True

time: 91.6 us -> 86.8 us (0.948)
  Pallas kernels: 86 us -> 81.2 us
    pallas_call x1, Pallas kernels: 86 us -> 81.2 us  [layer(): pl.pallas_call(layer_kernel, in_specs=[vmem] * 4, out_specs=[vmem] * 4, o...]
where the time goes in v4:
time: 86.8 us; the launch traced here: 86.6 us
  Pallas kernels  81.2 us (94%)
  local copies, waits for them, and re-layouts  4.76 us (5%)
    pallas_call x1, Pallas kernels, layer(): pl.pallas_call(layer_kernel, in_specs=[vmem] * 4, out_specs=[vmem] * 4, o...  81.2 us
    unnamed x10, local copies, waits for them, and re-layouts  4.76 us

profile of v4, /device:TPU:0, one launch (start us, length us, event | category | flops | bytes accessed | tf_op | source)
XLA Modules:
  0.0 86.6 jit_solution(6999555652593276702)
XLA Ops:
  0.6 81.2 %shard_map.75 = (bf16[1024,512]{1,0:T(8,128)(2,1)}, bf16[1024,512]{1,0:T(8,128)(2,1)}, f32[3,128,256]{2,1,0:T(8,128)}, f32[64,512]{1,0:T(8,128)}) custom-call(bf16[1024,1024]{1,0:T(8,128)(2,1)} %bitcast.8, bf16[1024,1024]{1,0:T(8,128)(2,1)} %bitcast.9, bf16[512,1024]{1,0:T(8,128)(2,1)} %merge_ref.1, bf16[3,1024,512]{2,1,0:T(8,128)(2,1)} %bitcast.7), custom_call_target="tpu_custom_call" | custom-call | tf_op jit(solution)/shard_map/pallas_call | solution.py:499
  81.8 0.0 copy-start
  81.8 0.0 copy-start.1
  81.8 0.0 copy-start.2
  81.8 2.4 %copy.12 = bf16[1,1024,512]{2,1,0:T(8,128)(2,1)} copy(bf16[1,1024,512]{2,1,0:T(8,128)(2,1)} %bitcast.11) | data formatting | bytes 2097152
  84.2 0.0 copy-done
  84.2 1.0 %copy.13 = bf16[1,1024,512]{2,1,0:T(8,128)(2,1)} copy(bf16[1,1024,512]{2,1,0:T(8,128)(2,1)S(1)} %bitcast.10) | data formatting | bytes 2097152
  85.2 0.0 copy-done.1
  85.2 0.7 copy.14
  85.9 0.0 copy-done.2
  85.9 0.7 copy.15
Async XLA Ops:
  81.8 2.4 %copy-start = (bf16[1024,512]{1,0:T(8,128)(2,1)S(1)}, bf16[1024,512]{1,0:T(8,128)(2,1)}, u32[]{:S(2)}) copy-start(bf16[1024,512]{1,0:T(8,128)(2,1)} %get-tuple-element.9) | copy-start | bytes 3145732
  81.8 3.4 %copy-start.1 = (f32[3,128,256]{2,1,0:T(8,128)S(1)}, f32[3,128,256]{2,1,0:T(8,128)}, u32[]{:S(2)}) copy-start(f32[3,128,256]{2,1,0:T(8,128)} %get-tuple-element.10) | copy-start | bytes 1179652
  81.8 4.1 %copy-start.2 = (f32[64,512]{1,0:T(8,128)S(1)}, f32[64,512]{1,0:T(8,128)}, u32[]{:S(2)}) copy-start(f32[64,512]{1,0:T(8,128)} %get-tuple-element.11) | copy-start | bytes 393220
